TPU v7x, 32 devices: a whole 2x2x4 slice. The times are simulated.
32 devices in a mesh: fsdp: 4 (over x, core), ctx: 2 (over y), tp: 4 (over z).
Axes of the slice: x: 2, y: 2, z: 4, core: 2. Of those that a mesh axis runs over, the one named last changes fastest.
Arguments:
- tokens: bfloat16 [4, 2048, 2048], P('fsdp', ('ctx', 'tp')), may hold values from -48 to 48
- segments: int32 [4, 2048], P('fsdp', 'ctx'), may hold values from 0 to 7, as said below
- positions: int32 [4, 2048], P('fsdp', 'ctx'), may hold values from 0 to 2047, as said below
- norm_gain: bfloat16 [2048], P(('fsdp', 'ctx')), may hold values from 0.25 to 1.75
- norm_bias: bfloat16 [2048], P(('fsdp', 'ctx')), may hold values from -3 to 3
- projection_weight: bfloat16 [2048, 3, 2048], P(('fsdp', 'ctx'), None, 'tp'), may hold values from -0.125 to 0.125
- projection_bias: bfloat16 [3, 2048], P(None, 'tp'), may hold values from -3 to 3
- dense_weight: bfloat16 [2048, 2048], P(('fsdp', 'ctx'), 'tp'), may hold values from -0.75 to 0.75
- dense_bias: bfloat16 [2048], P(('fsdp', 'ctx')), may hold values from -3 to 3
- up_weight: bfloat16 [2048, 8192], P(('fsdp', 'ctx'), 'tp'), may hold values from -0.125 to 0.125
- up_bias: bfloat16 [8192], P('tp'), may hold values from -3 to 3
- down_weight: bfloat16 [2048, 8192], P(('fsdp', 'ctx'), 'tp'), may hold values from -0.0625 to 0.0625
- down_bias: bfloat16 [2048], P(('fsdp', 'ctx')), may hold values from -3 to 3
- cotangent: bfloat16 [4, 2048, 2048], P('fsdp', ('ctx', 'tp')), may hold values from -6 to 6
Outputs:
- layer_output: bfloat16 [4, 2048, 2048], P('fsdp', ('ctx', 'tp'))
- input_grad: float32 [4, 2048, 2048], P('fsdp', ('ctx', 'tp'))
- norm_gain_grad: float32 [2048], P(('fsdp', 'ctx'))
- norm_bias_grad: float32 [2048], P(('fsdp', 'ctx'))
- projection_weight_grad: float32 [2048, 3, 2048], P(('fsdp', 'ctx'), None, 'tp')
- projection_bias_grad: float32 [3, 2048], P(None, 'tp')
- dense_weight_grad: float32 [2048, 2048], P(('fsdp', 'ctx'), 'tp')
- dense_bias_grad: float32 [2048], P(('fsdp', 'ctx'))
- up_weight_grad: float32 [2048, 8192], P(('fsdp', 'ctx'), 'tp')
- up_bias_grad: float32 [8192], P('tp')
- down_weight_grad: float32 [2048, 8192], P(('fsdp', 'ctx'), 'tp')
- down_bias_grad: float32 [2048], P(('fsdp', 'ctx'))
Inputs may be any that keep to these rules, and one draw needn't show every extreme that they name: `segments`: each sequence holds exactly 8 documents, numbered from 0 in order of place; the tokens at places 2048 // 4 to 1536 of every sequence lie in one document. A token's position counts from its document's first token, except in the first document of a sequence, whose positions run up to 2047 at its last token.
All inputs are finite; a program needn't handle non-finite values.
Results may differ from a plain program's by a relative error of at most 0.011.
Values may be sent and summed in bfloat16 or wider, within the bound.
A program may use at most 192 MiB of HBM per device.

v0:
```python
import math

import jax
import jax.numpy as jnp
from jax import lax
from jax.sharding import PartitionSpec as P

HD = 64
ROT = 32


epsilon = 1e-05
big_negative = -1000000000.0
root_two_over_pi = 0.7978845608028654
contract_rows = (((0,), (0,)), ((), ()))
contract_cols = (((1,), (1,)), ((), ()))


def shifted(value, axis, steps):
    count = lax.axis_size(axis)
    first, last = (max(0, -steps), min(count, count - steps))
    return lax.ppermute(value, axis, [(source, source + steps) for source in range(first, last)])


def layer_norm(values, gain_full, shift_full):
    center = jnp.mean(values, axis=-1, keepdims=True)
    centered = values - center
    spread = jnp.mean(centered * centered, axis=-1, keepdims=True)
    return centered * lax.rsqrt(spread + epsilon) * gain_full + shift_full


def gelu_new(values):
    return (
        0.5
        * values
        * (1.0 + jnp.tanh(root_two_over_pi * (values + 0.044715 * values * values * values)))
    )


def angles(position_row):
    exponent = jnp.arange(ROT // 2, dtype=jnp.float32) * 2.0 / ROT
    inverse = 10000.0 ** (-exponent)
    phase_angle = position_row.astype(jnp.float32)[..., None] * inverse
    return (jnp.cos(phase_angle), jnp.sin(phase_angle))


def rotate(values, cosine_table, sine_table):
    half_rot = ROT // 2
    leading = values[..., :half_rot]
    trailing = values[..., half_rot:ROT]
    return jnp.concatenate(
        [
            leading * cosine_table - trailing * sine_table,
            trailing * cosine_table + leading * sine_table,
            values[..., ROT:],
        ],
        axis=-1,
    )


def head_major(values, head_count):
    seq_count, length = (values.shape[0], values.shape[1])
    return (
        values.reshape(seq_count, length, head_count, HD)
        .transpose(0, 2, 1, 3)
        .reshape(seq_count * head_count, length, HD)
    )


def row_major(values, seq_count):
    item_count, length, head_size = values.shape
    head_count = item_count // seq_count
    return (
        values.reshape(seq_count, head_count, length, head_size)
        .transpose(0, 2, 1, 3)
        .reshape(seq_count, length, head_count * head_size)
    )


def body(
    tokens,
    segments,
    positions,
    norm_gain,
    norm_bias,
    projection_weight,
    projection_bias,
    dense_weight,
    dense_bias,
    up_weight,
    up_bias,
    down_weight,
    down_bias,
    cotangent,
):
    seq_count, own_len, model_width = tokens.shape
    half_len = segments.shape[1]
    rows_all = seq_count * half_len
    local_width = projection_weight.shape[2]
    head_count = local_width // HD
    hidden_width = up_weight.shape[1]
    shard_rows = norm_gain.shape[0]
    score_scale = 1.0 / math.sqrt(HD)
    has_prev = lax.axis_index("ctx") > 0
    block_rows = min(512, half_len)
    block_count = half_len // block_rows
    key_places = jnp.arange(half_len)
    gain_part, shift_part, bias_dense, bias_down = (
        lax.all_gather(norm_gain, ("fsdp", "ctx"), axis=0, tiled=True),
        lax.all_gather(norm_bias, ("fsdp", "ctx"), axis=0, tiled=True),
        lax.all_gather(dense_bias, ("fsdp", "ctx"), axis=0, tiled=True),
        lax.all_gather(down_bias, ("fsdp", "ctx"), axis=0, tiled=True),
    )
    gain_full = gain_part.astype(jnp.float32)
    shift_full = shift_part.astype(jnp.float32)
    inputs = tokens.astype(jnp.float32)
    normed_values, norm_pull = jax.vjp(layer_norm, inputs, gain_full, shift_full)
    normed = lax.all_gather(normed_values.astype(jnp.bfloat16), "tp", axis=1, tiled=True).reshape(
        rows_all, model_width
    )
    pieces = (
        lax.all_gather(projection_weight, ("fsdp", "ctx"), axis=0, tiled=True),
        lax.all_gather(up_weight, ("fsdp", "ctx"), axis=0, tiled=True),
    )
    count = pieces[0].shape[0]
    columns = normed
    projected = jnp.dot(
        columns, pieces[0].reshape(count, 3 * local_width), preferred_element_type=jnp.float32
    )
    hidden_pre = jnp.dot(columns, pieces[1], preferred_element_type=jnp.float32)
    projected = (projected + projection_bias.astype(jnp.float32).reshape(3 * local_width)).reshape(
        seq_count, half_len, 3, head_count, HD
    )
    hidden_pre = hidden_pre + up_bias.astype(jnp.float32)
    gelu_values, gelu_pull = jax.vjp(gelu_new, hidden_pre)
    activation = gelu_values.astype(jnp.bfloat16)
    cosine_table, sine_table = angles(positions)
    cosine_table = cosine_table[:, :, None, :]
    sine_table = sine_table[:, :, None, :]
    query_rows = (
        rotate(projected[:, :, 0], cosine_table, sine_table)
        .astype(jnp.bfloat16)
        .reshape(seq_count, half_len, local_width)
    )
    key_rows = (
        rotate(projected[:, :, 1], cosine_table, sine_table)
        .astype(jnp.bfloat16)
        .reshape(seq_count, half_len, local_width)
    )
    value_rows = projected[:, :, 2].astype(jnp.bfloat16).reshape(seq_count, half_len, local_width)
    prev_keys, prev_values, prev_segments = shifted((key_rows, value_rows, segments), "ctx", 1)
    query_items = head_major(query_rows, head_count)
    key_items = head_major(key_rows, head_count)
    value_items = head_major(value_rows, head_count)
    prev_key_items = head_major(prev_keys, head_count)
    prev_value_items = head_major(prev_values, head_count)
    segment_items = jnp.repeat(segments, head_count, axis=0)
    prev_segment_items = jnp.repeat(prev_segments, head_count, axis=0)

    def scores_for(
        query_block, query_segment, query_place, key_item, key_segment, prev_key_item, prev_segment
    ):
        own_scores = (
            jnp.dot(query_block, key_item.T, preferred_element_type=jnp.float32) * score_scale
        )
        own_ok = (query_segment[:, None] == key_segment[None, :]) & (
            key_places[None, :] <= query_place[:, None]
        )
        own_scores = jnp.where(own_ok, own_scores, big_negative)

        def cross_on():
            raw_scores = (
                jnp.dot(query_block, prev_key_item.T, preferred_element_type=jnp.float32)
                * score_scale
            )
            return jnp.where(
                query_segment[:, None] == prev_segment[None, :], raw_scores, big_negative
            )

        def cross_off():
            return jnp.full((block_rows, half_len), big_negative, jnp.float32)

        return (own_scores, lax.cond(has_prev, cross_on, cross_off))

    def attend(element):
        (
            query_item,
            key_item,
            value_item,
            prev_key_item,
            prev_value_item,
            segment_item,
            prev_segment,
        ) = element

        def block_step(number):
            offset = number * block_rows
            query_block = lax.dynamic_slice_in_dim(query_item, offset, block_rows, 0)
            query_segment = lax.dynamic_slice_in_dim(segment_item, offset, block_rows, 0)
            query_place = offset + jnp.arange(block_rows)
            own_scores, cross_scores = scores_for(
                query_block,
                query_segment,
                query_place,
                key_item,
                segment_item,
                prev_key_item,
                prev_segment,
            )
            highest = jnp.maximum(
                jnp.max(own_scores, axis=1, keepdims=True),
                jnp.max(cross_scores, axis=1, keepdims=True),
            )
            exp_own = jnp.exp(own_scores - highest)
            exp_cross = jnp.exp(cross_scores - highest)
            denominator = jnp.sum(exp_own, axis=1, keepdims=True) + jnp.sum(
                exp_cross, axis=1, keepdims=True
            )
            probs_own = (exp_own / denominator).astype(jnp.bfloat16)
            probs_cross = (exp_cross / denominator).astype(jnp.bfloat16)
            attended = jnp.dot(probs_own, value_item, preferred_element_type=jnp.float32)

            def cross_value():
                return attended + jnp.dot(
                    probs_cross, prev_value_item, preferred_element_type=jnp.float32
                )

            def cross_none():
                return attended

            attended = lax.cond(has_prev, cross_value, cross_none)
            return (attended.astype(jnp.bfloat16), (highest + jnp.log(denominator))[:, 0])

        attended, log_total = lax.map(block_step, jnp.arange(block_count))
        return (attended.reshape(half_len, HD), log_total.reshape(half_len))

    attended_items, log_items = lax.map(
        attend,
        (
            query_items,
            key_items,
            value_items,
            prev_key_items,
            prev_value_items,
            segment_items,
            prev_segment_items,
        ),
    )
    attended_rows = row_major(attended_items, seq_count).reshape(rows_all, local_width)
    pieces = (
        lax.all_gather(dense_weight, ("fsdp", "ctx"), axis=0, tiled=True),
        lax.all_gather(down_weight, ("fsdp", "ctx"), axis=0, tiled=True),
    )
    block_out = lax.dot_general(
        attended_rows, pieces[0], contract_cols, preferred_element_type=jnp.float32
    )
    block_out = block_out + lax.dot_general(
        activation, pieces[1], contract_cols, preferred_element_type=jnp.float32
    )
    branch_own = lax.psum_scatter(
        block_out.reshape(seq_count, half_len, model_width), "tp", scatter_dimension=1, tiled=True
    )
    layer_output = (
        inputs + branch_own + (bias_dense.astype(jnp.float32) + bias_down.astype(jnp.float32))
    ).astype(jnp.bfloat16)
    cotangent_own = cotangent.astype(jnp.float32)
    cotangent_rows = lax.all_gather(cotangent, "tp", axis=1, tiled=True).reshape(
        rows_all, model_width
    )
    pieces = (
        lax.all_gather(dense_weight, ("fsdp", "ctx"), axis=0, tiled=True),
        lax.all_gather(down_weight, ("fsdp", "ctx"), axis=0, tiled=True),
    )
    columns = cotangent_rows
    grad_attended = jnp.dot(columns, pieces[0], preferred_element_type=jnp.float32)
    grad_activation = jnp.dot(columns, pieces[1], preferred_element_type=jnp.float32)
    grad_attended = grad_attended.astype(jnp.bfloat16)
    grad_hidden = gelu_pull(grad_activation)[0].astype(jnp.bfloat16)
    grad_items = head_major(grad_attended.reshape(seq_count, half_len, local_width), head_count)

    def attend_back(element):
        (
            query_item,
            key_item,
            value_item,
            prev_key_item,
            prev_value_item,
            segment_item,
            prev_segment,
            log_item,
            grad_item,
        ) = element

        def block_step(running, number):
            offset = number * block_rows
            query_block = lax.dynamic_slice_in_dim(query_item, offset, block_rows, 0)
            query_segment = lax.dynamic_slice_in_dim(segment_item, offset, block_rows, 0)
            query_place = offset + jnp.arange(block_rows)
            log_block = lax.dynamic_slice_in_dim(log_item, offset, block_rows, 0)
            grad_block = lax.dynamic_slice_in_dim(grad_item, offset, block_rows, 0)
            own_scores, cross_scores = scores_for(
                query_block,
                query_segment,
                query_place,
                key_item,
                segment_item,
                prev_key_item,
                prev_segment,
            )
            probs_own = jnp.exp(own_scores - log_block[:, None])
            probs_cross = jnp.exp(cross_scores - log_block[:, None])
            dprob_own = jnp.dot(grad_block, value_item.T, preferred_element_type=jnp.float32)

            def cross_prob():
                return jnp.dot(grad_block, prev_value_item.T, preferred_element_type=jnp.float32)

            def cross_zero():
                return jnp.zeros_like(dprob_own)

            dprob_cross = lax.cond(has_prev, cross_prob, cross_zero)
            row_delta = jnp.sum(probs_own * dprob_own, axis=1, keepdims=True) + jnp.sum(
                probs_cross * dprob_cross, axis=1, keepdims=True
            )
            dscore_own = (probs_own * (dprob_own - row_delta)).astype(jnp.bfloat16)
            dscore_cross = (probs_cross * (dprob_cross - row_delta)).astype(jnp.bfloat16)
            back_query = jnp.dot(dscore_own, key_item, preferred_element_type=jnp.float32)
            back_key = lax.dot_general(
                dscore_own, query_block, contract_rows, preferred_element_type=jnp.float32
            )
            back_value = lax.dot_general(
                probs_own.astype(jnp.bfloat16),
                grad_block,
                contract_rows,
                preferred_element_type=jnp.float32,
            )

            def cross_terms():
                return (
                    jnp.dot(dscore_cross, prev_key_item, preferred_element_type=jnp.float32),
                    lax.dot_general(
                        dscore_cross, query_block, contract_rows, preferred_element_type=jnp.float32
                    ),
                    lax.dot_general(
                        probs_cross.astype(jnp.bfloat16),
                        grad_block,
                        contract_rows,
                        preferred_element_type=jnp.float32,
                    ),
                )

            def cross_none():
                return (
                    jnp.zeros((block_rows, HD), jnp.float32),
                    jnp.zeros((half_len, HD), jnp.float32),
                    jnp.zeros((half_len, HD), jnp.float32),
                )

            extra_query, far_key, far_value = lax.cond(has_prev, cross_terms, cross_none)
            own_key, own_value, sum_far_key, sum_far_value = running
            running = (
                own_key + back_key * score_scale,
                own_value + back_value,
                sum_far_key + far_key * score_scale,
                sum_far_value + far_value,
            )
            return (running, (back_query + extra_query) * score_scale)

        zero_rows = jnp.zeros((half_len, HD), jnp.float32)
        running, query_grads = lax.scan(
            block_step, (zero_rows, zero_rows, zero_rows, zero_rows), jnp.arange(block_count)
        )
        return (query_grads.reshape(half_len, HD), running[0], running[1], running[2], running[3])

    query_back, key_own, value_own, key_far, value_far = lax.map(
        attend_back,
        (
            query_items,
            key_items,
            value_items,
            prev_key_items,
            prev_value_items,
            segment_items,
            prev_segment_items,
            log_items,
            grad_items,
        ),
    )
    key_home, value_home = shifted(
        (row_major(key_far, seq_count), row_major(value_far, seq_count)), "ctx", -1
    )
    head_shape = (seq_count, half_len, head_count, HD)
    grad_query = rotate(
        row_major(query_back, seq_count).reshape(head_shape), cosine_table, -sine_table
    )
    grad_key = rotate(
        (row_major(key_own, seq_count) + key_home).reshape(head_shape), cosine_table, -sine_table
    )
    grad_value = (row_major(value_own, seq_count) + value_home).reshape(head_shape)
    grad_projected = (
        jnp.stack([grad_query, grad_key, grad_value], axis=2)
        .reshape(rows_all, 3 * local_width)
        .astype(jnp.bfloat16)
    )
    pieces = (
        lax.all_gather(projection_weight, ("fsdp", "ctx"), axis=0, tiled=True),
        lax.all_gather(up_weight, ("fsdp", "ctx"), axis=0, tiled=True),
    )
    count = pieces[0].shape[0]
    block_in = lax.dot_general(
        grad_projected,
        pieces[0].reshape(count, 3 * local_width),
        contract_cols,
        preferred_element_type=jnp.float32,
    )
    block_in = block_in + lax.dot_general(
        grad_hidden, pieces[1], contract_cols, preferred_element_type=jnp.float32
    )
    grad_normed_own = lax.psum_scatter(
        block_in.reshape(seq_count, half_len, model_width), "tp", scatter_dimension=1, tiled=True
    )
    grad_inputs, grad_gain, grad_shift = norm_pull(grad_normed_own)
    input_grad = grad_inputs + cotangent_own
    first_cut = 3 * local_width
    weight_grads = lax.psum_scatter(
        jnp.concatenate(
            [
                lax.dot_general(
                    normed, grad_projected, contract_rows, preferred_element_type=jnp.float32
                ),
                lax.dot_general(
                    cotangent_rows, attended_rows, contract_rows, preferred_element_type=jnp.float32
                ),
                lax.dot_general(
                    normed, grad_hidden, contract_rows, preferred_element_type=jnp.float32
                ),
                lax.dot_general(
                    cotangent_rows, activation, contract_rows, preferred_element_type=jnp.float32
                ),
            ],
            axis=1,
        ),
        ("fsdp", "ctx"),
        scatter_dimension=0,
        tiled=True,
    )
    second_cut = first_cut + local_width
    third_cut = second_cut + hidden_width
    projection_part = weight_grads[:, :first_cut]
    dense_part = weight_grads[:, first_cut:second_cut]
    up_part = weight_grads[:, second_cut:third_cut]
    down_part = weight_grads[:, third_cut:]
    tp_index = lax.axis_index("tp")
    tp_count = lax.axis_size("tp")
    projected_sum = jnp.sum(grad_projected.astype(jnp.float32), axis=0).reshape(3, local_width)
    hidden_sum = jnp.sum(grad_hidden.astype(jnp.float32), axis=0)
    output_sum = jnp.sum(cotangent_own, axis=(0, 1))
    projected_full = lax.dynamic_update_slice_in_dim(
        jnp.zeros((3, local_width * tp_count), jnp.float32),
        projected_sum,
        tp_index * local_width,
        1,
    )
    hidden_full = lax.dynamic_update_slice_in_dim(
        jnp.zeros((hidden_width * tp_count,), jnp.float32), hidden_sum, tp_index * hidden_width, 0
    )
    gain_total, shift_total, output_total, projected_total, hidden_total = lax.psum(
        (grad_gain, grad_shift, output_sum, projected_full, hidden_full), ("fsdp", "ctx", "tp")
    )
    shard_start = lax.axis_index(("fsdp", "ctx")) * shard_rows
    output_bias_grad = lax.dynamic_slice_in_dim(output_total, shard_start, shard_rows, 0)
    return (
        layer_output,
        input_grad,
        lax.dynamic_slice_in_dim(gain_total, shard_start, shard_rows, 0),
        lax.dynamic_slice_in_dim(shift_total, shard_start, shard_rows, 0),
        projection_part.reshape(shard_rows, 3, local_width),
        lax.dynamic_slice_in_dim(projected_total, tp_index * local_width, local_width, 1),
        dense_part,
        output_bias_grad,
        up_part,
        lax.dynamic_slice_in_dim(hidden_total, tp_index * hidden_width, hidden_width, 0),
        down_part,
        output_bias_grad,
    )


def solution(mesh):
    placed = (
        P("fsdp", ("ctx", "tp"), None),
        P("fsdp", "ctx"),
        P("fsdp", "ctx"),
        P(("fsdp", "ctx")),
        P(("fsdp", "ctx")),
        P(("fsdp", "ctx"), None, "tp"),
        P(None, "tp"),
        P(("fsdp", "ctx"), "tp"),
        P(("fsdp", "ctx")),
        P(("fsdp", "ctx"), "tp"),
        P("tp"),
        P(("fsdp", "ctx"), "tp"),
        P(("fsdp", "ctx")),
        P("fsdp", ("ctx", "tp"), None),
    )
    return jax.shard_map(
        body,
        mesh=mesh,
        in_specs=placed,
        out_specs=(
            P("fsdp", ("ctx", "tp"), None),
            P("fsdp", ("ctx", "tp"), None),
            P(("fsdp", "ctx")),
            P(("fsdp", "ctx")),
            P(("fsdp", "ctx"), None, "tp"),
            P(None, "tp"),
            P(("fsdp", "ctx"), "tp"),
            P(("fsdp", "ctx")),
            P(("fsdp", "ctx"), "tp"),
            P("tp"),
            P(("fsdp", "ctx"), "tp"),
            P(("fsdp", "ctx")),
        ),
        check_vma=False,
    )
```

profile of v0, /device:TPU:0, one launch (start us, length us, event | category | flops | bytes accessed | tf_op | source)
XLA Modules:
  0.0 1924.0 jit_solution(1215204383820960353)
XLA Ops:
  48.9 74.6 %all-gather.11.cloned.1.call-done = bf16[1,1024,2048]{2,1,0:T(8,128)(2,1)} async-done(((bf16[1,256,2048]{2,1,0:T(8,128)(2,1)}), bf16[1,1024,2048]{2,1,0:T(8,128)(2,1)}) %all-gather.11.cloned.1.call-update) | async-done | bytes 4194320 | tf_op jit(solution)/shard_map/all_gather | solution.py:118
  123.6 47.1 %all-gather.13.cloned.1.call-done = bf16[2048,3,512]{0,2,1:T(8,128)(2,1)} async-done(((bf16[256,3,512]{0,2,1:T(8,128)(2,1)}), bf16[2048,3,512]{0,2,1:T(8,128)(2,1)}) %all-gather.13.cloned.1.call-update) | async-done | bytes 6291472 | tf_op jit(solution)/shard_map/all_gather | solution.py:122
  201.6 81.1 %all-gather.21.cloned.1.call-done = bf16[1,1024,2048]{2,1,0:T(8,128)(2,1)} async-done(((bf16[1,256,2048]{2,1,0:T(8,128)(2,1)}), bf16[1,1024,2048]{2,1,0:T(8,128)(2,1)}) %all-gather.21.cloned.1.call-update) | async-done | bytes 4194320 | tf_op jit(solution)/shard_map/all_gather | solution.py:267
  307.2 253.3 %while.66 = (s32[]{:T(128)}, bf16[8,1024,64]{1,2,0:T(8,128)(2,1)}, f32[8,1024]{1,0:T(8,128)}, bf16[8,1024,64]{2,1,0:T(8,128)(2,1)}, s32[8,1024]{1,0:T(8,128)}, /...) while((s32[]{:T(128)}, bf16[8,1024,64]{1,2,0:T(8,128)(2,1)}, ...), condition=%wide.region_13.14_spmd.clone, body=%wide.region_2.13_spmd.clone.sunk | while | flops 278987264 | bytes 26702612 | solution.py:237
  313.0 22.1 %while.69 = (s32[]{:T(128)}, bf16[2,512,64]{1,2,0:T(8,128)(2,1)}, f32[2,512]{1,0:T(2,128)}, pred[]{:T(512)}, s32[2]{0:T(128)}, /*index=5*/s32[1024]{0:T(1024)S(1...) while((s32[]{:T(128)}, bf16[2,512,64]{1,2,0:T(8,128)(2,1)}, ...), condition=%wide.region_12.12_spmd, body=%wide.region_3.11_spmd.sunk | while | flops 278987264 | bytes 24568256 | solution.py:234
  344.8 22.0 %while.69 = (s32[]{:T(128)}, bf16[2,512,64]{1,2,0:T(8,128)(2,1)}, f32[2,512]{1,0:T(2,128)}, pred[]{:T(512)}, s32[2]{0:T(128)}, /*index=5*/s32[1024]{0:T(1024)S(1...) while((s32[]{:T(128)}, bf16[2,512,64]{1,2,0:T(8,128)(2,1)}, ...), condition=%wide.region_12.12_spmd, body=%wide.region_3.11_spmd.sunk | while | flops 278987264 | bytes 24568256 | solution.py:234
  376.5 22.0 %while.69 = (s32[]{:T(128)}, bf16[2,512,64]{1,2,0:T(8,128)(2,1)}, f32[2,512]{1,0:T(2,128)}, pred[]{:T(512)}, s32[2]{0:T(128)}, /*index=5*/s32[1024]{0:T(1024)S(1...) while((s32[]{:T(128)}, bf16[2,512,64]{1,2,0:T(8,128)(2,1)}, ...), condition=%wide.region_12.12_spmd, body=%wide.region_3.11_spmd.sunk | while | flops 278987264 | bytes 24568256 | solution.py:234
  408.2 22.0 %while.69 = (s32[]{:T(128)}, bf16[2,512,64]{1,2,0:T(8,128)(2,1)}, f32[2,512]{1,0:T(2,128)}, pred[]{:T(512)}, s32[2]{0:T(128)}, /*index=5*/s32[1024]{0:T(1024)S(1...) while((s32[]{:T(128)}, bf16[2,512,64]{1,2,0:T(8,128)(2,1)}, ...), condition=%wide.region_12.12_spmd, body=%wide.region_3.11_spmd.sunk | while | flops 278987264 | bytes 24568256 | solution.py:234
  439.8 22.0 %while.69 = (s32[]{:T(128)}, bf16[2,512,64]{1,2,0:T(8,128)(2,1)}, f32[2,512]{1,0:T(2,128)}, pred[]{:T(512)}, s32[2]{0:T(128)}, /*index=5*/s32[1024]{0:T(1024)S(1...) while((s32[]{:T(128)}, bf16[2,512,64]{1,2,0:T(8,128)(2,1)}, ...), condition=%wide.region_12.12_spmd, body=%wide.region_3.11_spmd.sunk | while | flops 278987264 | bytes 24568256 | solution.py:234
  471.4 22.0 %while.69 = (s32[]{:T(128)}, bf16[2,512,64]{1,2,0:T(8,128)(2,1)}, f32[2,512]{1,0:T(2,128)}, pred[]{:T(512)}, s32[2]{0:T(128)}, /*index=5*/s32[1024]{0:T(1024)S(1...) while((s32[]{:T(128)}, bf16[2,512,64]{1,2,0:T(8,128)(2,1)}, ...), condition=%wide.region_12.12_spmd, body=%wide.region_3.11_spmd.sunk | while | flops 278987264 | bytes 24568256 | solution.py:234
  503.0 22.0 %while.69 = (s32[]{:T(128)}, bf16[2,512,64]{1,2,0:T(8,128)(2,1)}, f32[2,512]{1,0:T(2,128)}, pred[]{:T(512)}, s32[2]{0:T(128)}, /*index=5*/s32[1024]{0:T(1024)S(1...) while((s32[]{:T(128)}, bf16[2,512,64]{1,2,0:T(8,128)(2,1)}, ...), condition=%wide.region_12.12_spmd, body=%wide.region_3.11_spmd.sunk | while | flops 278987264 | bytes 24568256 | solution.py:234
  534.6 22.0 %while.69 = (s32[]{:T(128)}, bf16[2,512,64]{1,2,0:T(8,128)(2,1)}, f32[2,512]{1,0:T(2,128)}, pred[]{:T(512)}, s32[2]{0:T(128)}, /*index=5*/s32[1024]{0:T(1024)S(1...) while((s32[]{:T(128)}, bf16[2,512,64]{1,2,0:T(8,128)(2,1)}, ...), condition=%wide.region_12.12_spmd, body=%wide.region_3.11_spmd.sunk | while | flops 278987264 | bytes 24568256 | solution.py:234
  560.5 385.3 %while.68 = (s32[]{:T(128)}, f32[8,1024,64]{1,2,0:T(8,128)}, f32[8,1024,64]{1,2,0:T(8,128)}, f32[8,1024,64]{1,2,0:T(8,128)}, f32[8,1024,64]{1,2,0:T(8,128)}, /*i...) while((s32[]{:T(128)}, f32[8,1024,64]{1,2,0:T(8,128)}, ...), condition=%wide.region_26.27_spmd.clone, body=%wide.region_15.26_spmd.clone.sunk | while | flops 683343872 | bytes 60761328 | solution.py:374
  572.9 32.0 %while.70 = (s32[]{:T(128)}, f32[1024,64]{0,1:T(8,128)}, f32[1024,64]{0,1:T(8,128)}, f32[1024,64]{0,1:T(8,128)}, f32[1024,64]{0,1:T(8,128)}, /*index=5*/f32[2,51...) while((s32[]{:T(128)}, f32[1024,64]{0,1:T(8,128)}, ...), condition=%wide.region_25.25_spmd.clone, body=%wide.region_16.24_spmd.clone.sunk | while | flops 683343872 | bytes 51294916 | solution.py:369
  621.0 32.0 %while.70 = (s32[]{:T(128)}, f32[1024,64]{0,1:T(8,128)}, f32[1024,64]{0,1:T(8,128)}, f32[1024,64]{0,1:T(8,128)}, f32[1024,64]{0,1:T(8,128)}, /*index=5*/f32[2,51...) while((s32[]{:T(128)}, f32[1024,64]{0,1:T(8,128)}, ...), condition=%wide.region_25.25_spmd.clone, body=%wide.region_16.24_spmd.clone.sunk | while | flops 683343872 | bytes 51294916 | solution.py:369
  669.2 32.0 %while.70 = (s32[]{:T(128)}, f32[1024,64]{0,1:T(8,128)}, f32[1024,64]{0,1:T(8,128)}, f32[1024,64]{0,1:T(8,128)}, f32[1024,64]{0,1:T(8,128)}, /*index=5*/f32[2,51...) while((s32[]{:T(128)}, f32[1024,64]{0,1:T(8,128)}, ...), condition=%wide.region_25.25_spmd.clone, body=%wide.region_16.24_spmd.clone.sunk | while | flops 683343872 | bytes 51294916 | solution.py:369
  717.3 32.0 %while.70 = (s32[]{:T(128)}, f32[1024,64]{0,1:T(8,128)}, f32[1024,64]{0,1:T(8,128)}, f32[1024,64]{0,1:T(8,128)}, f32[1024,64]{0,1:T(8,128)}, /*index=5*/f32[2,51...) while((s32[]{:T(128)}, f32[1024,64]{0,1:T(8,128)}, ...), condition=%wide.region_25.25_spmd.clone, body=%wide.region_16.24_spmd.clone.sunk | while | flops 683343872 | bytes 51294916 | solution.py:369
  765.5 32.0 %while.70 = (s32[]{:T(128)}, f32[1024,64]{0,1:T(8,128)}, f32[1024,64]{0,1:T(8,128)}, f32[1024,64]{0,1:T(8,128)}, f32[1024,64]{0,1:T(8,128)}, /*index=5*/f32[2,51...) while((s32[]{:T(128)}, f32[1024,64]{0,1:T(8,128)}, ...), condition=%wide.region_25.25_spmd.clone, body=%wide.region_16.24_spmd.clone.sunk | while | flops 683343872 | bytes 51294916 | solution.py:369
  813.7 32.0 %while.70 = (s32[]{:T(128)}, f32[1024,64]{0,1:T(8,128)}, f32[1024,64]{0,1:T(8,128)}, f32[1024,64]{0,1:T(8,128)}, f32[1024,64]{0,1:T(8,128)}, /*index=5*/f32[2,51...) while((s32[]{:T(128)}, f32[1024,64]{0,1:T(8,128)}, ...), condition=%wide.region_25.25_spmd.clone, body=%wide.region_16.24_spmd.clone.sunk | while | flops 683343872 | bytes 51294916 | solution.py:369
  861.8 32.0 %while.70 = (s32[]{:T(128)}, f32[1024,64]{0,1:T(8,128)}, f32[1024,64]{0,1:T(8,128)}, f32[1024,64]{0,1:T(8,128)}, f32[1024,64]{0,1:T(8,128)}, /*index=5*/f32[2,51...) while((s32[]{:T(128)}, f32[1024,64]{0,1:T(8,128)}, ...), condition=%wide.region_25.25_spmd.clone, body=%wide.region_16.24_spmd.clone.sunk | while | flops 683343872 | bytes 51294916 | solution.py:369
  910.0 32.0 %while.70 = (s32[]{:T(128)}, f32[1024,64]{0,1:T(8,128)}, f32[1024,64]{0,1:T(8,128)}, f32[1024,64]{0,1:T(8,128)}, f32[1024,64]{0,1:T(8,128)}, /*index=5*/f32[2,51...) while((s32[]{:T(128)}, f32[1024,64]{0,1:T(8,128)}, ...), condition=%wide.region_25.25_spmd.clone, body=%wide.region_16.24_spmd.clone.sunk | while | flops 683343872 | bytes 51294916 | solution.py:369
  950.1 136.8 %collective-permute-done.3 = f32[1,1024,512]{1,2,0:T(8,128)S(1)} collective-permute-done((f32[1,1024,512]{1,2,0:T(8,128)}, f32[1,1024,512]{1,2,0:T(8,128)S(1)}, u32[]{:S(2)}, u32[]{:S(2)}) %collective-permute-start.3) | collective-permute-done | bytes 2097184 | tf_op jit(solution)/shard_map/ppermute | solution.py:22
  1089.8 41.5 %collective-permute-done.4 = f32[1,1024,512]{1,2,0:T(8,128)S(1)} collective-permute-done((f32[1,1024,512]{1,2,0:T(8,128)}, f32[1,1024,512]{1,2,0:T(8,128)S(1)}, u32[]{:S(2)}, u32[]{:S(2)}) %collective-permute-start.4) | collective-permute-done | bytes 2097184 | tf_op jit(solution)/shard_map/ppermute | solution.py:22
  1132.4 14.5 fusion.31
  1147.0 19.8 %convert_reduce_fusion = (f32[2048]{0:T(1024)S(1)}, bf16[1024,2048]{1,0:T(8,128)(2,1)S(1)}) fusion(bf16[2048,2048]{1,0:T(8,128)(2,1)} %all-gather.19.cloned.1.call-done, bf16[1,1024,2048]{2,1,0:T(8,128)(2,1)} %all-gather.21.cloned.1.call-done, f32[1024,2048]{1,0:T(8,128)} %fusion.31, f32[2048]{0:T(1024)S(1)} %convert_element_type.177), kind=kOutput, calls=%fused_computation.72 | convolution fusion | flops 8646555648 | bytes 25182208 | tf_op jit(solution)/shard_map/dot_general | solution.py:276
  1189.0 16.4 fusion.59
  1225.1 14.3 all-gather.2
  1282.7 48.2 %reduce-scatter.6.cloned.1.call-done = f32[1,256,2048]{2,1,0:T(8,128)} async-done(((f32[1,1024,2048]{2,1,0:T(8,128)}), f32[1,256,2048]{2,1,0:T(8,128)}) %reduce-scatter.6.cloned.1.call-update) | async-done | bytes 2097168 | tf_op jit(solution)/shard_map/reduce_scatter | solution.py:418
  1335.2 143.2 %reduce-scatter.4.cloned.1.call-done = f32[1,256,2048]{2,1,0:T(8,128)} async-done(((f32[1,1024,2048]{2,1,0:T(8,128)}), f32[1,256,2048]{2,1,0:T(8,128)}) %reduce-scatter.4.cloned.1.call-update) | async-done | bytes 2097168 | tf_op jit(solution)/shard_map/reduce_scatter | solution.py:260
  1484.1 34.2 %pad_maximum_fusion = f32[2048,6144]{0,1:T(8,128)} fusion(f32[2048,2048]{0,1:T(8,128)} %convolution_bitcast_fusion, f32[2048,2048]{0,1:T(8,128)} %fusion.27, f32[2048,512]{0,1:T(8,128)} %fusion.34, f32[2048,1536]{0,1:T(8,128)} %fusion.29), kind=kLoop, calls=%fused_computation.60 | loop fusion | flops 37748736 | bytes 100663296 | tf_op jit(solution)/shard_map/concatenate | solution.py:425
  1518.3 90.8 %all-reduce.3.cloned.1.call-done = (f32[2048]{0:T(1024)}, f32[2048]{0:T(1024)}, f32[3,2048]{1,0:T(4,128)}, f32[2048]{0:T(1024)}, f32[8192]{0:T(1024)}) async-done(((f32[2048]{0:T(1024)}, f32[2048]{0:T(1024)}, f32[3,2048]{1,0:T(4,128)}, f32[2048]{0:T(1024)}, f32[8192]{0:T(1024)}), (f32[2048]{0:T(1024)}, f32[2048]{0:T(1024)}, f32[3,2048]{1,0:T(4,128)}, f32[2048]{0:T(1024)}, ...) | async-done | bytes 81936 | tf_op jit(solution)/shard_map/psum | solution.py:466
  1615.1 284.7 %reduce-scatter.8.cloned.1.call-done = f32[256,6144]{0,1:T(8,128)} async-done(((f32[2048,6144]{0,1:T(8,128)}), f32[256,6144]{0,1:T(8,128)}) %reduce-scatter.8.cloned.1.call-update) | async-done | bytes 6291472 | tf_op jit(solution)/shard_map/reduce_scatter | solution.py:424
  (1633 shorter events, 879.3 us)
Async XLA Ops:
  7.2 33.1 %copy-start.13 = (bf16[1,256,2048]{2,1,0:T(8,128)(2,1)S(1)}, bf16[1,256,2048]{2,1,0:T(8,128)(2,1)}, u32[]{:S(2)}) copy-start(bf16[1,256,2048]{2,1,0:T(8,128)(2,1)} %param.32) | copy-start | bytes 3145732
  7.2 116.4 %all-gather.11.cloned.1.call-start = ((), (), s32[]{:S(2)}) async-start(), calls=%async_computation.3 | async-start | bytes 5242880 | tf_op jit(solution)/shard_map/all_gather | solution.py:118
  10.1 29.6 %copy-start.32 = (f32[256]{0:T(256)}, f32[256]{0:T(256)S(1)}, u32[]{:S(2)}) copy-start(f32[256]{0:T(256)S(1)} %broadcast_multiply_fusion) | copy-start | bytes 3076
  10.1 31.7 %copy-start.23 = (bf16[256,3,512]{2,0,1:T(8,128)(2,1)S(1)}, bf16[256,3,512]{2,0,1:T(8,128)(2,1)}, u32[]{:S(2)}) copy-start(bf16[256,3,512]{2,0,1:T(8,128)(2,1)} %param.37) | copy-start | bytes 2359300
  12.4 27.3 %copy-start.34 = (f32[256]{0:T(256)}, f32[256]{0:T(256)S(1)}, u32[]{:S(2)}) copy-start(f32[256]{0:T(256)S(1)} %fusion.57) | copy-start | bytes 3076
  41.8 128.9 %all-gather.13.cloned.1.call-start = ((), (), s32[]{:S(2)}) async-start(), calls=%async_computation.4 | async-start | bytes 7077888 | tf_op jit(solution)/shard_map/all_gather | solution.py:122
  43.0 158.5 %all-gather.15.cloned.1.call-start = ((), (), s32[]{:S(2)}) async-start(), calls=%async_computation.5 | async-start | bytes 2359296 | tf_op jit(solution)/shard_map/all_gather | solution.py:251
  43.7 239.0 %all-gather.21.cloned.1.call-start = ((), (), s32[]{:S(2)}) async-start(), calls=%async_computation.9 | async-start | bytes 5242880 | tf_op jit(solution)/shard_map/all_gather | solution.py:267
  44.3 1088.1 %all-gather.17.cloned.1.call-start = ((), (), s32[]{:S(2)}) async-start(), calls=%async_computation.6 | async-start | bytes 9437184 | tf_op jit(solution)/shard_map/all_gather | solution.py:123
  44.9 1102.1 %all-gather.19.cloned.1.call-start = ((), (), s32[]{:S(2)}) async-start(), calls=%async_computation.7 | async-start | bytes 9437184 | tf_op jit(solution)/shard_map/all_gather | solution.py:252
  45.0 261.0 %collective-permute-start.1 = (s32[1,1024]{1,0:T(1,128)S(1)}, s32[1,1024]{1,0:T(1,128)S(1)}, u32[]{:S(2)}, u32[]{:S(2)}) collective-permute-start(s32[1,1024]{1,0:T(1,128)S(1)} %copy-done.39), channel_id=1, source_target_pairs={{0,4},{1,5},{2,6},{3,7},{8,12},{9,13},{10,14},{11,15},{16,20},{17,... | collective-permute-start | bytes 12296 | tf_op jit(solution)/shard_map/ppermute | solution.py:22
  47.8 1283.1 %reduce-scatter.6.cloned.1.call-start = ((), (), s32[]{:S(2)}) async-start(), calls=%async_computation.10 | async-start | bytes 10485760 | tf_op jit(solution)/shard_map/reduce_scatter | solution.py:418
  48.9 244.1 %copy-start.21 = (f32[1024,16]{0,1:T(8,128)}, f32[1024,16]{0,1:T(8,128)S(1)}, u32[]{:S(2)}) copy-start(f32[1024,16]{0,1:T(8,128)S(1)} %get-tuple-element.837) | copy-start | bytes 196612
  195.9 104.5 %collective-permute-start = (bf16[1,1024,512]{1,2,0:T(8,128)(2,1)}, bf16[1,1024,512]{1,2,0:T(8,128)(2,1)}, u32[]{:S(2)}, u32[]{:S(2)}) collective-permute-start(bf16[1,1024,512]{1,2,0:T(8,128)(2,1)} %bitcast.18), channel_id=1, source_target_pairs={{0,4},{1,5},{2,6},{3,7},{8,12},{9,13},{10,14},{11,15},{16,20},{17,... | collective-permute-start | bytes 3145736 | tf_op jit(solution)/shard_map/ppermute | solution.py:22
  199.3 103.8 %collective-permute-start.2 = (bf16[1,1024,512]{1,2,0:T(8,128)(2,1)}, bf16[1,1024,512]{1,2,0:T(8,128)(2,1)}, u32[]{:S(2)}, u32[]{:S(2)}) collective-permute-start(bf16[1,1024,512]{1,2,0:T(8,128)(2,1)} %bitcast.26), channel_id=1, source_target_pairs={{0,4},{1,5},{2,6},{3,7},{8,12},{9,13},{10,14},{11,15},{16,20},{17,... | collective-permute-start | bytes 3145736 | tf_op jit(solution)/shard_map/ppermute | solution.py:22
  560.5 388.3 %copy-start.40 = (bf16[2048]{0:T(1024)(128)(2,1)S(1)}, bf16[2048]{0:T(1024)(128)(2,1)}, u32[]{:S(2)}) copy-start(bf16[2048]{0:T(1024)(128)(2,1)} %param.42) | copy-start | bytes 12292
  945.8 141.1 %collective-permute-start.3 = (f32[1,1024,512]{1,2,0:T(8,128)}, f32[1,1024,512]{1,2,0:T(8,128)S(1)}, u32[]{:S(2)}, u32[]{:S(2)}) collective-permute-start(f32[1,1024,512]{1,2,0:T(8,128)} %bitcast.324), channel_id=1, source_target_pairs={{4,0},{5,1},{6,2},{7,3},{12,8},{13,9},{14,10},{15,11},{20,16},{21,... | collective-permute-start | bytes 6291464 | tf_op jit(solution)/shard_map/ppermute | solution.py:22
  947.1 184.1 %collective-permute-start.4 = (f32[1,1024,512]{1,2,0:T(8,128)}, f32[1,1024,512]{1,2,0:T(8,128)S(1)}, u32[]{:S(2)}, u32[]{:S(2)}) collective-permute-start(f32[1,1024,512]{1,2,0:T(8,128)} %bitcast.323), channel_id=1, source_target_pairs={{4,0},{5,1},{6,2},{7,3},{12,8},{13,9},{14,10},{15,11},{20,16},{21,... | collective-permute-start | bytes 6291464 | tf_op jit(solution)/shard_map/ppermute | solution.py:22
  1089.5 41.7 %copy-start.19 = (f32[8,1024,64]{1,2,0:T(8,128)S(1)}, f32[8,1024,64]{1,2,0:T(8,128)}, u32[]{:S(2)}) copy-start(f32[8,1024,64]{1,2,0:T(8,128)} %get-tuple-element.414) | copy-start | bytes 6291460
  1166.7 13.1 copy-start.49
  1189.0 289.5 %reduce-scatter.4.cloned.1.call-start = ((), (), s32[]{:S(2)}) async-start(), calls=%async_computation.8 | async-start | bytes 10485760 | tf_op jit(solution)/shard_map/reduce_scatter | solution.py:260
  1189.0 16.5 copy-start.45
  1189.0 16.5 copy-start.46
  1211.3 397.9 %all-reduce.3.cloned.1.call-start = ((), (), s32[]{:S(2)}) async-start(), calls=%async_computation.12 | async-start | bytes 180224 | tf_op jit(solution)/shard_map/psum | solution.py:466
  1246.3 23.9 %slice-start.2 = ((s8[8388608]{0:T(1024)(128)(4,1)}), s8[4194304]{0:T(1024)(128)(4,1)S(1)}, s32[]{:S(2)}) async-start(s8[8388608]{0:T(1024)(128)(4,1)} %bitcast.327), calls=%async_computation.15 | async-start | bytes 8388608
  1270.3 60.6 %copy-start.14 = (bf16[1,256,2048]{2,1,0:T(8,128)(2,1)S(1)}, bf16[1,256,2048]{2,1,0:T(8,128)(2,1)}, u32[]{:S(2)}) copy-start(bf16[1,256,2048]{2,1,0:T(8,128)(2,1)} %param.32) | copy-start | bytes 3145732
  1270.3 60.6 %copy-start.26 = (f32[8,1,256]{2,1,0:T(1,128)S(1)}, f32[8,1,256]{2,1,0:T(1,128)}, u32[]{:S(2)}) copy-start(f32[8,1,256]{2,1,0:T(1,128)} %copy-done.25) | copy-start | bytes 24580
  1270.3 60.6 %copy-start.33 = (f32[256]{0:T(256)S(1)}, f32[256]{0:T(256)}, u32[]{:S(2)}) copy-start(f32[256]{0:T(256)} %copy-done.32) | copy-start | bytes 3076
  1282.7 51.1 %copy-start.37 = (f32[256]{0:T(256)S(1)}, f32[256]{0:T(256)}, u32[]{:S(2)}) copy-start(f32[256]{0:T(256)} %copy-done.36) | copy-start | bytes 3076
  1282.7 51.1 %copy-start.35 = (f32[256]{0:T(256)S(1)}, f32[256]{0:T(256)}, u32[]{:S(2)}) copy-start(f32[256]{0:T(256)} %copy-done.34) | copy-start | bytes 3076
  1484.0 415.9 %reduce-scatter.8.cloned.1.call-start = ((), (), s32[]{:S(2)}) async-start(), calls=%async_computation.11 | async-start | bytes 56623104 | tf_op jit(solution)/shard_map/reduce_scatter | solution.py:424
  1611.2 304.9 %copy-start.42 = (f32[256]{0:T(256)}, f32[256]{0:T(256)S(1)}, u32[]{:S(2)}) copy-start(f32[256]{0:T(256)S(1)} %dynamic_slice.94) | copy-start | bytes 3076
  (276 other events, 513.9 us)
Sparse Core Ops, SparseCore 0:
  41.9 81.6 all-gather.10
  125.4 45.1 all-gather.12
  172.6 27.8 all-gather.14
  201.9 80.7 all-gather.20
  284.4 52.9 all-gather.16
  339.1 54.4 all-gather.18
  1189.1 141.7 reduce-scatter.5
  1333.2 145.2 reduce-scatter.3
  1486.1 123.0 all-reduce.2
  1612.6 287.1 reduce-scatter.7
where the time goes:
time: 1940 us; the launch traced here: 1920 us
  waiting for transfers between devices  950 us (49%)
  local copies, waits for them, and re-layouts  416 us (21%)
  matrix products  280 us (14%)
  other arithmetic  170 us (9%)
  blocking collectives  54.7 us (3%)
  loops' own time  26 us (1%)
    reduce_scatter x1, waiting for transfers between devices, body(): lax.psum_scatter(jnp.concatenate([lax.dot_general(normed, grad_projected,...  285 us
    ppermute x5, waiting for transfers between devices, shifted(): lax.ppermute(value, axis, [(source, source + steps) for source in range(f...  178 us
    reduce_scatter x1, waiting for transfers between devices, body(): lax.psum_scatter(block_out.reshape(seq_count, half_len, model_width), 'tp...  143 us
    squeeze x72, local copies, waits for them, and re-layouts, body(): lax.map(attend, (query_items, key_items, value_items, prev_key_items, pre...  105 us
    psum x1, waiting for transfers between devices, body(): lax.psum((grad_gain, grad_shift, output_sum, projected_full, hidden_full)...  90.8 us
    all_gather x1, waiting for transfers between devices, body(): lax.all_gather(cotangent, 'tp', axis=1, tiled=True)  81.1 us
    all_gather x1, waiting for transfers between devices, body(): lax.all_gather(normed_values.astype(jnp.bfloat16), 'tp', axis=1, tiled=True)  74.6 us
    dot_general x32, matrix products, scores_for(): jnp.dot(query_block, key_item.T, preferred_element_type=jnp.float32)  72.7 us
  transfers between devices with their start and end apart: 15, of which 9 were waited for; matrix products, arithmetic and copies ran while one was open for 39% of the time, Pallas kernels for 0%

commit v1 on v0

v1 whole, which is shorter than its diff:
```python
import functools
import math

import jax
import jax.numpy as jnp
from jax import lax
from jax.experimental import pallas as pl
from jax.experimental.pallas import tpu as pltpu
from jax.sharding import PartitionSpec as P

HD = 64
ROT = 32
TILE = 256

epsilon = 1e-05
big_negative = -1000000000.0
root_two_over_pi = 0.7978845608028654
contract_rows = (((0,), (0,)), ((), ()))
contract_cols = (((1,), (1,)), ((), ()))
row_by_col = (((0,), (1,)), ((), ()))
MESH = pl.DeviceIdType.MESH
ANY = pl.BlockSpec(memory_space=pl.ANY)
VMEM = pl.BlockSpec(memory_space=pltpu.VMEM)
SMEM = pl.BlockSpec(memory_space=pltpu.SMEM)
DMA = pltpu.SemaphoreType.DMA
f32 = jnp.float32
bf16 = jnp.bfloat16


def layer_norm(values, gain_full, shift_full):
    center = jnp.mean(values, axis=-1, keepdims=True)
    centered = values - center
    spread = jnp.mean(centered * centered, axis=-1, keepdims=True)
    return centered * lax.rsqrt(spread + epsilon) * gain_full + shift_full


def gelu_new(values):
    return (
        0.5
        * values
        * (1.0 + jnp.tanh(root_two_over_pi * (values + 0.044715 * values * values * values)))
    )


class Place:
    def __init__(self, sizes):
        self.chips = sizes["fsdp"] // 2
        self.halves = sizes["ctx"]
        self.depth = sizes["tp"]
        lane = lax.axis_index("fsdp")
        self.chip = lane // 2
        self.core = lane % 2
        self.half = lax.axis_index("ctx")
        self.layer = lax.axis_index("tp")

    def device(self, chip=None, core=None, half=None, layer=None):
        chip = self.chip if chip is None else chip
        core = self.core if core is None else core
        half = self.half if half is None else half
        layer = self.layer if layer is None else layer
        return (chip * 2 + core, half, layer)

    def block(self, chip=None, core=None, half=None):
        chip = self.chip if chip is None else chip
        core = self.core if core is None else core
        half = self.half if half is None else half
        return (chip * 2 + core) * self.halves + half

    def ahead(self, k):
        return (self.chip + k) % self.chips

    def behind(self, k):
        return (self.chip + self.chips - k) % self.chips

    def pair(self):
        return self.device(core=1 - self.core)

    def across(self):
        return self.device(half=1 - self.half)

    def group(self):
        found = []
        for k in range(self.chips):
            for core in range(2):
                for half in range(2):
                    if k or core or half:
                        found.append(
                            (self.ahead(k), (self.core + core) % 2, (self.half + half) % 2)
                        )
        return found


def greet(devices):
    barrier = pltpu.get_barrier_semaphore()
    for device in devices:
        pl.semaphore_signal(barrier, inc=1, device_id=device, device_id_type=MESH)
    pl.semaphore_wait(barrier, len(devices))


def greet_line(place, devices):
    barrier = pltpu.get_barrier_semaphore()
    for device in devices:
        pl.semaphore_signal(barrier, inc=1, device_id=device, device_id_type=MESH)
    up, down = place.layer < place.depth - 1, place.layer > 0

    @pl.when(up)
    def _():
        pl.semaphore_signal(
            barrier, inc=1, device_id=place.device(layer=place.layer + 1), device_id_type=MESH
        )

    @pl.when(down)
    def _():
        pl.semaphore_signal(
            barrier, inc=1, device_id=place.device(layer=place.layer - 1), device_id_type=MESH
        )

    pl.semaphore_wait(barrier, len(devices) + up.astype(jnp.int32) + down.astype(jnp.int32))


def send(source, target, send_sem, recv_sem, device):
    return pltpu.make_async_remote_copy(
        src_ref=source,
        dst_ref=target,
        send_sem=send_sem,
        recv_sem=recv_sem,
        device_id=device,
        device_id_type=MESH,
    )


def plane(place):
    found = [place.device(chip=place.ahead(k)) for k in range(1, place.chips)]
    return found + [place.across(), place.pair()]


def small_gather(sizes, block, pairs):
    count = sizes["fsdp"] * sizes["ctx"]

    def kernel(block_ref, pair_ref, full_ref, other_ref, send_sem, recv_sem, keep_sem, swap_sem):
        place = Place(sizes)
        peers = place.group()
        greet([place.device(chip=a, core=b, half=c) for a, b, c in peers])
        mine = place.block()
        keep = pltpu.make_async_copy(block_ref, full_ref.at[mine], keep_sem)
        keep.start()
        swap = send(pair_ref, other_ref, swap_sem.at[0], swap_sem.at[1], place.across())
        swap.start()
        copies = []
        for at, (chip, core, half) in enumerate(peers):
            copy = send(
                block_ref,
                full_ref.at[mine],
                send_sem.at[at],
                recv_sem.at[at],
                place.device(chip=chip, core=core, half=half),
            )
            copy.start()
            copies.append(copy)
        keep.wait()
        for at, copy in enumerate(copies):
            k, core, half = at_of(at)
            source = place.block(
                place.behind(k), (place.core + core) % 2, (place.half + half) % 2
            )
            copy.wait_send()
            send(
                block_ref, full_ref.at[source], send_sem.at[at], recv_sem.at[at], place.pair()
            ).wait_recv()
        swap.wait()

    def at_of(at):
        return (at + 1) // 4, ((at + 1) // 2) % 2, (at + 1) % 2

    return pl.pallas_call(
        kernel,
        out_shape=(
            jax.ShapeDtypeStruct((count,) + block.shape, block.dtype),
            jax.ShapeDtypeStruct(pairs.shape, pairs.dtype),
        ),
        in_specs=[VMEM, VMEM],
        out_specs=(VMEM, VMEM),
        scratch_shapes=[DMA((count - 1,)), DMA((count - 1,)), DMA, DMA((2,))],
        compiler_params=pltpu.CompilerParams(collective_id=0, has_side_effects=True),
        name="small_gather",
    )(block, pairs)


def gather(sizes, lines, weights, collective_id, name):
    chips, halves, depth = sizes["fsdp"] // 2, sizes["ctx"], sizes["tp"]
    line_count, weight_count = len(lines), len(weights)

    def kernel(*refs):
        refs = list(refs)

        def take(count):
            taken = refs[:count]
            del refs[:count]
            return taken

        line_in, weight_in = take(line_count), take(weight_count)
        line_out, weight_out = take(line_count), take(weight_count)
        keep, line_send, line_recv, near_send, near_recv = take(5)
        turn_send, turn_recv, core_send, core_recv = take(4)
        place = Place(sizes)
        up, down = place.layer < depth - 1, place.layer > 0
        greet_line(place, plane(place))

        def part(ref, block, rows, first=0, count=None):
            count = rows if count is None else count
            start = pl.multiple_of(block * rows + first, 16)
            return ref.at[pl.ds(start, count)]

        pending = []

        def launch(copy, condition=None):
            if condition is None:
                copy.start()
            else:
                pl.when(condition)(copy.start)
            pending.append((copy, condition))

        for a in range(line_count):
            rows = line_in[a].shape[0]
            own = part(line_out[a], place.layer, rows)
            for way, (step, condition) in enumerate(((1, up), (-1, down))):
                launch(
                    send(
                        line_in[a],
                        own,
                        line_send.at[a, way, 0],
                        line_recv.at[a, way, 0],
                        place.device(layer=jnp.clip(place.layer + step, 0, depth - 1)),
                    ),
                    condition,
                )
        for a in range(weight_count):
            rows = weight_in[a].shape[0]
            own = part(weight_out[a], place.block(), rows)
            for k in range(1, chips):
                launch(
                    send(
                        weight_in[a],
                        own,
                        near_send.at[a, k],
                        near_recv.at[a, k],
                        place.device(chip=place.ahead(k)),
                    )
                )
            launch(
                send(weight_in[a], own, near_send.at[a, 0], near_recv.at[a, 0], place.across())
            )
            launch(send(weight_in[a], own, core_send.at[a, 0], core_recv.at[a, 0], place.pair()))
        kept = []
        for a in range(line_count):
            rows = line_in[a].shape[0]
            kept.append(
                pltpu.make_async_copy(
                    line_in[a], part(line_out[a], place.layer, rows), keep.at[a]
                )
            )
        for a in range(weight_count):
            rows = weight_in[a].shape[0]
            kept.append(
                pltpu.make_async_copy(
                    weight_in[a],
                    part(weight_out[a], place.block(), rows),
                    keep.at[line_count + a],
                )
            )
        for copy in kept:
            copy.start()

        def line_step(k):
            for a in range(line_count):
                rows = line_in[a].shape[0]
                for way, step in enumerate((1, -1)):
                    source = place.layer - step * k
                    there = (source >= 0) & (source < depth)
                    source = jnp.clip(source, 0, depth - 1)
                    piece = part(line_out[a], source, rows)
                    target = place.layer + step
                    onward = there & (target >= 0) & (target < depth)
                    device = place.device(layer=jnp.clip(target, 0, depth - 1))
                    arrived = send(
                        piece,
                        piece,
                        line_send.at[a, way, k - 1],
                        line_recv.at[a, way, k - 1],
                        device,
                    )
                    pl.when(there)(arrived.wait_recv)
                    if k < depth - 1:
                        launch(
                            send(
                                piece,
                                piece,
                                line_send.at[a, way, k],
                                line_recv.at[a, way, k],
                                device,
                            ),
                            onward,
                        )

        def near_step():
            for a in range(weight_count):
                rows = weight_in[a].shape[0]
                side = rows // 2
                for k in range(1, chips):
                    block = place.block(chip=place.behind(k))
                    piece = part(weight_out[a], block, rows)
                    send(
                        piece, piece, near_send.at[a, k], near_recv.at[a, k], place.pair()
                    ).wait_recv()
                    top = part(weight_out[a], block, rows, 0, side)
                    launch(
                        send(
                            top, top, turn_send.at[a, 0, k], turn_recv.at[a, 0, k], place.across()
                        )
                    )
                    launch(
                        send(piece, piece, core_send.at[a, k], core_recv.at[a, k], place.pair())
                    )
                block = place.block(half=1 - place.half)
                piece = part(weight_out[a], block, rows)
                send(
                    piece, piece, near_send.at[a, 0], near_recv.at[a, 0], place.pair()
                ).wait_recv()
                low = part(weight_out[a], block, rows, side, side)
                for k in range(1, chips):
                    launch(
                        send(
                            low,
                            low,
                            turn_send.at[a, 1, k],
                            turn_recv.at[a, 1, k],
                            place.device(chip=place.ahead(k)),
                        )
                    )
                launch(
                    send(
                        piece, piece, core_send.at[a, chips], core_recv.at[a, chips], place.pair()
                    )
                )

        def turn_step():
            for a in range(weight_count):
                rows = weight_in[a].shape[0]
                side = rows // 2
                for k in range(1, chips):
                    block = place.block(chip=place.behind(k), half=1 - place.half)
                    for number in range(2):
                        piece = part(weight_out[a], block, rows, number * side, side)
                        send(
                            piece,
                            piece,
                            turn_send.at[a, number, k],
                            turn_recv.at[a, number, k],
                            place.pair(),
                        ).wait_recv()
                    piece = part(weight_out[a], block, rows)
                    launch(
                        send(
                            piece,
                            piece,
                            core_send.at[a, chips + k],
                            core_recv.at[a, chips + k],
                            place.pair(),
                        )
                    )

        def core_step():
            other = 1 - place.core
            for a in range(weight_count):
                rows = weight_in[a].shape[0]
                blocks = [place.block(core=other)]
                blocks += [place.block(place.behind(k), other) for k in range(1, chips)]
                blocks += [place.block(None, other, 1 - place.half)]
                blocks += [
                    place.block(place.behind(k), other, 1 - place.half) for k in range(1, chips)
                ]
                for at, block in enumerate(blocks):
                    piece = part(weight_out[a], block, rows)
                    send(
                        piece, piece, core_send.at[a, at], core_recv.at[a, at], place.pair()
                    ).wait_recv()

        line_step(1)
        near_step()
        for k in range(2, depth):
            line_step(k)
        turn_step()
        core_step()
        for copy in kept:
            copy.wait()
        for copy, condition in pending:
            if condition is None:
                copy.wait_send()
            else:
                pl.when(condition)(copy.wait_send)

    count = sizes["fsdp"] * halves
    shapes = [jax.ShapeDtypeStruct((depth * v.shape[0], v.shape[1]), v.dtype) for v in lines]
    shapes += [jax.ShapeDtypeStruct((count * v.shape[0], v.shape[1]), v.dtype) for v in weights]
    return pl.pallas_call(
        kernel,
        out_shape=tuple(shapes),
        in_specs=[ANY] * (line_count + weight_count),
        out_specs=(ANY,) * (line_count + weight_count),
        scratch_shapes=[
            DMA((line_count + weight_count,)),
            DMA((line_count, 2, depth - 1)),
            DMA((line_count, 2, depth - 1)),
            DMA((weight_count, chips)),
            DMA((weight_count, chips)),
            DMA((weight_count, 2, chips)),
            DMA((weight_count, 2, chips)),
            DMA((weight_count, 2 * chips)),
            DMA((weight_count, 2 * chips)),
        ],
        compiler_params=pltpu.CompilerParams(collective_id=collective_id, has_side_effects=True),
        name=name,
    )(*lines, *weights)


def reduce(sizes, line, weights, small, collective_id, name):
    chips, halves, depth = sizes["fsdp"] // 2, sizes["ctx"], sizes["tp"]
    groups = chips * halves
    weight_count = len(weights)
    line_rows, line_width = line.shape[0] // depth, line.shape[1]
    block_rows = weights[0].shape[0] // (2 * groups)
    widths = [v.shape[1] for v in weights]
    side = block_rows // 2
    has_small = small is not None

    def kernel(*refs):
        refs = list(refs)

        def take(count):
            taken = refs[:count]
            del refs[:count]
            return taken

        (line_ref,) = take(1)
        weight_in = take(weight_count)
        small_ref = take(1)[0] if has_small else None
        (line_out,) = take(1)
        weight_out = take(weight_count)
        small_out = take(1)[0] if has_small else None
        flow, fresh = take(2)
        own, pair, turn_a, turn_b, near = (take(weight_count) for _ in range(5))
        line_send, line_recv, load_sem, core_send, core_recv = take(5)
        turn_send, turn_recv, near_send, near_recv = take(4)
        if has_small:
            small_pair, small_near, small_far, small_send, small_recv = take(5)
        place = Place(sizes)
        greet_line(place, plane(place))
        pending = []

        def launch(copy, condition=None):
            if condition is None:
                copy.start()
            else:
                pl.when(condition)(copy.start)
            pending.append((copy, condition))

        other = 1 - place.core
        for a in range(weight_count):
            for number in range(groups):
                chip, half = number // halves, number % halves
                theirs = place.block(chip, other, half)
                mine = place.block(chip, place.core, half)
                launch(
                    send(
                        weight_in[a].at[
                            pl.ds(pl.multiple_of(theirs * block_rows, 16), block_rows)
                        ],
                        pair[a].at[number],
                        core_send.at[a, number],
                        core_recv.at[a, number],
                        place.pair(),
                    )
                )
                pltpu.make_async_copy(
                    weight_in[a].at[pl.ds(pl.multiple_of(mine * block_rows, 16), block_rows)],
                    own[a].at[number],
                    load_sem.at[a, number],
                ).start()

        def line_ends(way, owner):
            step = 1 if way == 0 else -1
            inner = (place.layer - owner) * step < 0
            first = place.layer == (0 if way == 0 else depth - 1)
            return step, inner, first

        def line_sum(way, hop):
            step = 1 if way == 0 else -1
            owner = depth - 1 - hop if way == 0 else hop
            sends = place.layer < owner if way == 0 else place.layer > owner
            first = place.layer == (0 if way == 0 else depth - 1)
            device = place.device(layer=jnp.clip(place.layer + step, 0, depth - 1))
            rows = line_ref.at[pl.ds(owner * line_rows, line_rows)]

            @pl.when(sends & jnp.logical_not(first))
            def _():
                send(
                    rows, flow.at[way, owner], line_send.at[way, owner], line_recv.at[way, owner], device
                ).wait_recv()

                @pl.loop(0, line_rows, step=16)
                def _(r):
                    at = pl.ds(pl.multiple_of(r, 16), 16)
                    start = pl.ds(pl.multiple_of(owner * line_rows + r, 16), 16)
                    total = line_ref[start, :].astype(f32) + flow[way, owner, at, :].astype(f32)
                    fresh[way, owner, at, :] = total.astype(bf16)

                send(
                    fresh.at[way, owner],
                    flow.at[way, owner],
                    line_send.at[way, owner],
                    line_recv.at[way, owner],
                    device,
                ).start()

            @pl.when(sends & first)
            def _():
                send(
                    rows, flow.at[way, owner], line_send.at[way, owner], line_recv.at[way, owner], device
                ).start()

            pending.append(
                (
                    send(
                        rows,
                        flow.at[way, owner],
                        line_send.at[way, owner],
                        line_recv.at[way, owner],
                        device,
                    ),
                    sends,
                )
            )

        def line_own():
            below, above = place.layer > 0, place.layer < depth - 1
            mine = place.layer
            rows = line_ref.at[pl.ds(pl.multiple_of(mine * line_rows, 16), line_rows)]
            for way, condition in ((0, below), (1, above)):
                pl.when(condition)(
                    send(
                        rows,
                        flow.at[way, mine],
                        line_send.at[way, mine],
                        line_recv.at[way, mine],
                        place.pair(),
                    ).wait_recv
                )

            @pl.loop(0, line_rows, step=16)
            def _(r):
                at = pl.ds(pl.multiple_of(r, 16), 16)
                start = pl.ds(pl.multiple_of(mine * line_rows + r, 16), 16)
                line_out[at, :] = line_ref[start, :].astype(f32)

            for way, condition in ((0, below), (1, above)):

                @pl.when(condition)
                def _(way=way):
                    @pl.loop(0, line_rows, step=16)
                    def _(r):
                        at = pl.ds(pl.multiple_of(r, 16), 16)
                        line_out[at, :] += flow[way, mine, at, :].astype(f32)

        def pair_sum(a, number):
            mine = own[a].at[number]
            theirs = pair[a].at[number]
            pltpu.make_async_copy(mine, mine, load_sem.at[a, number]).wait()
            send(
                theirs, theirs, core_send.at[a, number], core_recv.at[a, number], place.pair()
            ).wait_recv()

            @pl.loop(0, block_rows, step=16)
            def _(r):
                at = pl.ds(pl.multiple_of(r, 16), 16)
                mine[at, :] = (mine[at, :].astype(f32) + theirs[at, :].astype(f32)).astype(bf16)

        def diagonal(a):
            for k in range(1, chips):
                number = place.ahead(k) * halves + 1 - place.half
                pair_sum(a, number)
                launch(
                    send(
                        own[a].at[number, pl.ds(0, side)],
                        turn_a[a].at[k - 1],
                        turn_send.at[a, 0, k],
                        turn_recv.at[a, 0, k],
                        place.across(),
                    )
                )
                launch(
                    send(
                        own[a].at[number, pl.ds(side, side)],
                        turn_b[a].at[k - 1],
                        turn_send.at[a, 1, k],
                        turn_recv.at[a, 1, k],
                        place.device(chip=place.ahead(k)),
                    )
                )

        def direct_pairs(a):
            for k in range(1, chips):
                pair_sum(a, place.ahead(k) * halves + place.half)
            pair_sum(a, place.chip * halves + 1 - place.half)

        def add_turn(a, number, first, refs_at):
            @pl.loop(0, side, step=16)
            def _(r):
                at = pl.ds(pl.multiple_of(first + r, 16), 16)
                total = own[a][number, at, :].astype(f32)
                for ref, k in refs_at:
                    total += ref[k, pl.ds(pl.multiple_of(r, 16), 16), :].astype(f32)
                own[a][number, at, :] = total.astype(bf16)

        def direct(a):
            for k in range(1, chips):
                number = place.ahead(k) * halves + place.half
                piece = turn_a[a].at[k - 1]
                send(
                    piece, piece, turn_send.at[a, 0, k], turn_recv.at[a, 0, k], place.across()
                ).wait_recv()
                add_turn(a, number, 0, [(turn_a[a], k - 1)])
                launch(
                    send(
                        own[a].at[number],
                        near[a].at[k],
                        near_send.at[a, k],
                        near_recv.at[a, k],
                        place.device(chip=place.ahead(k)),
                    )
                )
            for k in range(1, chips):
                piece = turn_b[a].at[k - 1]
                send(
                    piece, piece, turn_send.at[a, 1, k], turn_recv.at[a, 1, k], place.across()
                ).wait_recv()
            number = place.chip * halves + 1 - place.half
            add_turn(a, number, side, [(turn_b[a], k - 1) for k in range(1, chips)])
            launch(
                send(
                    own[a].at[number],
                    near[a].at[0],
                    near_send.at[a, 0],
                    near_recv.at[a, 0],
                    place.across(),
                )
            )

        def finish(a):
            for k in range(chips):
                piece = near[a].at[k]
                send(
                    piece, piece, near_send.at[a, k], near_recv.at[a, k], place.across()
                ).wait_recv()
            number = place.chip * halves + place.half

            @pl.loop(0, block_rows, step=16)
            def _(r):
                at = pl.ds(pl.multiple_of(r, 16), 16)
                total = own[a][number, at, :].astype(f32) + near[a][0, at, :].astype(f32)
                for k in range(1, chips):
                    total += near[a][k, at, :].astype(f32)
                weight_out[a][at, :] = total

        def swap_small(source, target, at, device):
            copy = send(source, target, small_send.at[at], small_recv.at[at], device)
            launch(copy)
            return copy

        for way in range(2):
            line_sum(way, 0)
        if has_small:
            swap_small(small_ref, small_pair, 0, place.pair())
        for a in range(weight_count):
            diagonal(a)
        for way in range(2):
            line_sum(way, 1)
        for a in range(weight_count):
            direct_pairs(a)
        if has_small:
            send(
                small_pair, small_pair, small_send.at[0], small_recv.at[0], place.pair()
            ).wait_recv()
            small_near[0] = small_ref[...] + small_pair[...]
            for k in range(1, chips):
                swap_small(
                    small_near.at[0], small_near.at[k], k, place.device(chip=place.ahead(k))
                )
        for a in range(weight_count):
            direct(a)
        for hop in range(2, depth - 1):
            for way in range(2):
                line_sum(way, hop)
        if has_small:
            total = small_near[0]
            for k in range(1, chips):
                piece = small_near.at[k]
                send(piece, piece, small_send.at[k], small_recv.at[k], place.pair()).wait_recv()
                total += small_near[k]
            small_far[0] = total
            swap_small(small_far.at[0], small_far.at[1], chips, place.across())
        for a in range(weight_count):
            pair_sum(a, place.chip * halves + place.half)
        for a in range(weight_count):
            finish(a)
        if has_small:
            piece = small_far.at[1]
            send(
                piece, piece, small_send.at[chips], small_recv.at[chips], place.pair()
            ).wait_recv()
            small_out[...] = small_far[0] + small_far[1]
        line_own()
        for copy, condition in pending:
            if condition is None:
                copy.wait_send()
            else:
                pl.when(condition)(copy.wait_send)

    shapes = [jax.ShapeDtypeStruct((line_rows, line_width), f32)]
    shapes += [jax.ShapeDtypeStruct((block_rows, w), f32) for w in widths]
    scratch = [
        pltpu.VMEM((2, depth, line_rows, line_width), bf16),
        pltpu.VMEM((2, depth, line_rows, line_width), bf16),
    ]
    for rows in ((groups, block_rows), (groups, block_rows), (chips - 1, side), (chips - 1, side)):
        scratch += [pltpu.VMEM(rows + (w,), bf16) for w in widths]
    scratch += [pltpu.VMEM((chips, block_rows, w), bf16) for w in widths]
    scratch += [
        DMA((2, depth)),
        DMA((2, depth)),
        DMA((weight_count, groups)),
        DMA((weight_count, groups)),
        DMA((weight_count, groups)),
        DMA((weight_count, 2, chips)),
        DMA((weight_count, 2, chips)),
        DMA((weight_count, chips)),
        DMA((weight_count, chips)),
    ]
    arguments = [line, *weights]
    in_specs = [VMEM] + [ANY] * weight_count
    if has_small:
        shapes.append(jax.ShapeDtypeStruct(small.shape, f32))
        scratch += [
            pltpu.VMEM(small.shape, f32),
            pltpu.VMEM((chips,) + small.shape, f32),
            pltpu.VMEM((2,) + small.shape, f32),
            DMA((chips + 1,)),
            DMA((chips + 1,)),
        ]
        arguments.append(small)
        in_specs.append(VMEM)
    return pl.pallas_call(
        kernel,
        out_shape=tuple(shapes),
        in_specs=in_specs,
        out_specs=(VMEM,) * len(shapes),
        scratch_shapes=scratch,
        compiler_params=pltpu.CompilerParams(
            collective_id=collective_id, has_side_effects=True, vmem_limit_bytes=60 << 20
        ),
        name=name,
    )(*arguments)


def small_reduce(sizes, blocks):
    count, depth = sizes["fsdp"] * sizes["ctx"], sizes["tp"]

    def kernel(blocks_ref, out_ref, landed, line, send_sem, recv_sem, line_send, line_recv):
        place = Place(sizes)
        peers = place.group()
        layers = [(place.layer + k) % depth for k in range(1, depth)]
        devices = [place.device(chip=a, core=b, half=c) for a, b, c in peers]
        greet(devices + [place.device(layer=k) for k in layers])
        copies = []
        for at, (chip, core, half) in enumerate(peers):
            copy = send(
                blocks_ref.at[place.block(chip, core, half)],
                landed.at[at],
                send_sem.at[at],
                recv_sem.at[at],
                devices[at],
            )
            copy.start()
            copies.append(copy)
        total = blocks_ref[place.block()]
        for at, copy in enumerate(copies):
            copy.wait()
            total += landed[at]
        line[0] = total
        copies = []
        for k, layer in enumerate(layers):
            copy = send(
                line.at[0],
                line.at[k + 1],
                line_send.at[k],
                line_recv.at[k],
                place.device(layer=layer),
            )
            copy.start()
            copies.append(copy)
        for k, copy in enumerate(copies):
            copy.wait()
            total += line[k + 1]
        out_ref[...] = total

    block = blocks.shape[1:]
    return pl.pallas_call(
        kernel,
        out_shape=jax.ShapeDtypeStruct(block, f32),
        in_specs=[VMEM],
        out_specs=VMEM,
        scratch_shapes=[
            pltpu.VMEM((count - 1,) + block, f32),
            pltpu.VMEM((depth,) + block, f32),
            DMA((count - 1,)),
            DMA((count - 1,)),
            DMA((depth - 1,)),
            DMA((depth - 1,)),
        ],
        compiler_params=pltpu.CompilerParams(collective_id=5, has_side_effects=True),
        name="small_reduce",
    )(blocks)


def attention_kernel(
    low_ref,
    mid_ref,
    first_ref,
    second_ref,
    grad_first_ref,
    grad_second_ref,
    start_ref,
    cosine_ref,
    sine_ref,
    attended_ref,
    back_ref,
    query_t,
    key_t,
    value_t,
    grad_t,
    key_rows,
    value_rows,
    scores,
    probs,
    key_sum,
    value_sum,
):
    length = first_ref.shape[2]
    total_length = 2 * length
    score_scale = 1.0 / math.sqrt(HD)
    for number, ref in enumerate((query_t, key_t, value_t)):
        scale = score_scale if number == 0 else 1.0
        for part, source in enumerate((first_ref, second_ref)):
            piece = source[number]
            ref[:, part * length : (part + 1) * length] = piece * scale if number == 0 else piece
    grad_t[:, :length] = grad_first_ref[...]
    grad_t[:, length:] = grad_second_ref[...]
    key_rows[...] = key_t[...].T
    value_rows[...] = value_t[...].T
    key_sum[...] = jnp.zeros_like(key_sum)
    value_sum[...] = jnp.zeros_like(value_sum)

    def turned_back(values, cosine, sine):
        half_rot = ROT // 2
        leading = values[:half_rot]
        trailing = values[half_rot:ROT]
        return jnp.concatenate(
            [
                leading * cosine + trailing * sine,
                trailing * cosine - leading * sine,
                values[ROT:],
            ],
            axis=0,
        )

    @pl.loop(0, total_length // TILE)
    def _(j):
        here = pl.ds(pl.multiple_of(j * TILE, TILE), TILE)
        query = query_t[:, here]
        grad = grad_t[:, here]
        start = start_ref[:, here]
        low, mid = low_ref[j], mid_ref[j]

        def at(kb):
            return pl.ds(pl.multiple_of(kb * TILE, TILE), TILE)

        def plain(kb, highest):
            found = jnp.dot(key_rows[at(kb), :], query, preferred_element_type=f32)
            scores[at(kb), :] = found
            return jnp.maximum(highest, jnp.max(found, axis=0, keepdims=True))

        def masked(kb, highest):
            found = jnp.dot(key_rows[at(kb), :], query, preferred_element_type=f32)
            places = kb * TILE + lax.broadcasted_iota(jnp.int32, (TILE, TILE), 0)
            own = j * TILE + lax.broadcasted_iota(jnp.int32, (TILE, TILE), 1)
            found = jnp.where((places >= start) & (places <= own), found, big_negative)
            scores[at(kb), :] = found
            return jnp.maximum(highest, jnp.max(found, axis=0, keepdims=True))

        highest = jnp.full((1, TILE), big_negative, f32)
        highest = lax.fori_loop(low, mid, masked, highest)
        highest = lax.fori_loop(mid, j, plain, highest)
        highest = masked(j, highest)

        def weigh(kb, carry):
            total, mixed = carry
            prob = jnp.exp(scores[at(kb), :] - highest)
            total = total + jnp.sum(prob, axis=0, keepdims=True)
            prob = prob.astype(bf16)
            probs[at(kb), :] = prob
            mixed = mixed + jnp.dot(value_t[:, at(kb)], prob, preferred_element_type=f32)
            return total, mixed

        total, mixed = lax.fori_loop(
            low, j + 1, weigh, (jnp.zeros((1, TILE), f32), jnp.zeros((HD, TILE), f32))
        )
        over = 1.0 / total
        mixed = mixed * over
        attended_ref[:, here] = mixed.astype(bf16)
        grad_wide = grad.astype(f32)
        delta = jnp.sum(grad_wide * mixed, axis=0, keepdims=True)
        query_over = (query.astype(f32) * over).T.astype(bf16)
        grad_over = (grad_wide * over).T.astype(bf16)

        def pull(kb, query_back):
            prob = probs[at(kb), :]
            down = jnp.dot(value_rows[at(kb), :], grad, preferred_element_type=f32)
            score_back = (prob.astype(f32) * (down - delta)).astype(bf16)
            value_sum[at(kb), :] += jnp.dot(prob, grad_over, preferred_element_type=f32)
            key_sum[at(kb), :] += jnp.dot(score_back, query_over, preferred_element_type=f32)
            return query_back + jnp.dot(
                key_t[:, at(kb)], score_back, preferred_element_type=f32
            )

        query_back = lax.fori_loop(low, j + 1, pull, jnp.zeros((HD, TILE), f32))
        query_back = query_back * (over * score_scale)
        back_ref[0, :, here] = turned_back(
            query_back, cosine_ref[:, here], sine_ref[:, here]
        ).astype(bf16)

    back_ref[1] = turned_back(key_sum[...].T, cosine_ref[...], sine_ref[...]).astype(bf16)
    back_ref[2] = value_sum[...].T.astype(bf16)


def attention(low, mid, first, second, grad_first, grad_second, start, cosine, sine):
    width, length = first.shape[1], first.shape[2]
    total = 2 * length
    heads = width // HD
    spec = pl.BlockSpec((3, HD, length), lambda h: (0, h, 0))
    grad_spec = pl.BlockSpec((HD, length), lambda h: (h, 0))
    whole = lambda rows: pl.BlockSpec((rows, total), lambda h: (0, 0))
    area = total * total // 2 * heads
    return pl.pallas_call(
        attention_kernel,
        grid=(heads,),
        out_shape=(
            jax.ShapeDtypeStruct((width, total), bf16),
            jax.ShapeDtypeStruct((3, width, total), bf16),
        ),
        in_specs=[
            SMEM,
            SMEM,
            spec,
            spec,
            grad_spec,
            grad_spec,
            whole(1),
            whole(ROT // 2),
            whole(ROT // 2),
        ],
        out_specs=(
            pl.BlockSpec((HD, total), lambda h: (h, 0)),
            pl.BlockSpec((3, HD, total), lambda h: (0, h, 0)),
        ),
        scratch_shapes=[
            pltpu.VMEM((HD, total), bf16),
            pltpu.VMEM((HD, total), bf16),
            pltpu.VMEM((HD, total), bf16),
            pltpu.VMEM((HD, total), bf16),
            pltpu.VMEM((total, HD), bf16),
            pltpu.VMEM((total, HD), bf16),
            pltpu.VMEM((total, TILE), f32),
            pltpu.VMEM((total, TILE), bf16),
            pltpu.VMEM((total, HD), f32),
            pltpu.VMEM((total, HD), f32),
        ],
        compiler_params=pltpu.CompilerParams(vmem_limit_bytes=40 << 20),
        cost_estimate=pl.CostEstimate(
            flops=10 * area * HD, bytes_accessed=8 * width * total, transcendentals=area
        ),
        name="attention",
    )(low, mid, first, second, grad_first, grad_second, start, cosine, sine)


def rotate_rows(values, cosine, sine):
    half_rot = ROT // 2
    leading = values[:, :half_rot]
    trailing = values[:, half_rot:ROT]
    return jnp.concatenate(
        [
            leading * cosine - trailing * sine,
            trailing * cosine + leading * sine,
            values[:, ROT:],
        ],
        axis=1,
    )


def body(
    sizes,
    tokens,
    segments,
    positions,
    norm_gain,
    norm_bias,
    projection_weight,
    projection_bias,
    dense_weight,
    dense_bias,
    up_weight,
    up_bias,
    down_weight,
    down_bias,
    cotangent,
):
    own_len, model_width = tokens.shape[1], tokens.shape[2]
    half_len = segments.shape[1]
    local_width = projection_weight.shape[2]
    hidden_width = up_weight.shape[1]
    shard_rows = norm_gain.shape[0]
    half_width = local_width // 2
    half = lax.axis_index("ctx")
    total_len = 2 * half_len
    swap = [(0, 1), (1, 0)]

    vectors = jnp.stack([norm_gain, norm_bias, dense_bias, down_bias]).astype(f32)
    vectors = jnp.pad(vectors, ((0, 4), (0, 0)))
    numbers = jnp.pad(jnp.concatenate([segments, positions], axis=0), ((0, 6), (0, 0)))
    vectors_full, numbers_other = small_gather(sizes, vectors, numbers)
    gain_full, shift_full, bias_dense, bias_down = (
        vectors_full[:, row].reshape(model_width) for row in range(4)
    )

    def in_order(own, other, axis):
        return jnp.where(
            half == 0,
            jnp.concatenate([own, other], axis=axis),
            jnp.concatenate([other, own], axis=axis),
        )

    sequence = in_order(numbers, numbers_other, 1)
    segment_row, position_row = sequence[0], sequence[1]
    places = jnp.arange(total_len, dtype=jnp.int32)
    edges = jnp.concatenate([jnp.ones((1,), bool), segment_row[1:] != segment_row[:-1]])
    start = lax.cummax(jnp.where(edges, places, 0))
    tile_count = total_len // TILE
    low = start[::TILE] // TILE
    mid = jnp.minimum(
        jnp.maximum((start[TILE - 1 :: TILE] + TILE - 1) // TILE, low),
        jnp.arange(tile_count, dtype=jnp.int32),
    )
    exponent = jnp.arange(ROT // 2, dtype=f32) * 2.0 / ROT
    inverse = 10000.0 ** (-exponent)
    phase_angle = inverse[:, None] * position_row.astype(f32)[None, :]
    cosine_full, sine_full = jnp.cos(phase_angle), jnp.sin(phase_angle)
    own_start = half * half_len
    cosine_own = lax.dynamic_slice_in_dim(cosine_full, own_start, half_len, 1)
    sine_own = lax.dynamic_slice_in_dim(sine_full, own_start, half_len, 1)

    inputs = tokens[0].astype(f32)
    normed_values, norm_pull = jax.vjp(layer_norm, inputs, gain_full, shift_full)
    normed, projection, up_full = gather(
        sizes,
        [normed_values.astype(bf16)],
        [projection_weight.reshape(shard_rows, 3 * local_width), up_weight],
        1,
        "gather_first",
    )
    cotangent_rows, dense_full, down_full = gather(
        sizes, [cotangent[0]], [dense_weight, down_weight], 2, "gather_second"
    )
    projected = lax.dot_general(projection, normed, row_by_col, preferred_element_type=f32)
    projected = projected + projection_bias.astype(f32).reshape(3 * local_width)[:, None]
    projected = projected.reshape(3, local_width, half_len)
    turned = rotate_rows(
        projected[:2].reshape(2 * local_width // HD, HD, half_len), cosine_own, sine_own
    ).reshape(2, local_width, half_len)
    triple = jnp.concatenate([turned, projected[2:]], axis=0).astype(bf16)

    def keep_and_swap(values, axis, width):
        kept = lax.dynamic_slice_in_dim(values, half * width, width, axis)
        sent = lax.dynamic_slice_in_dim(values, (1 - half) * width, width, axis)
        return kept, lax.ppermute(sent, "ctx", swap)

    kept, came = keep_and_swap(triple, 1, half_width)
    first = jnp.where(half == 0, kept, came)
    second = jnp.where(half == 0, came, kept)

    hidden_pre = jnp.dot(normed, up_full, preferred_element_type=f32) + up_bias.astype(f32)
    gelu_values, gelu_pull = jax.vjp(gelu_new, hidden_pre)
    activation = gelu_values.astype(bf16)

    grad_attended = lax.dot_general(
        dense_full, cotangent_rows, row_by_col, preferred_element_type=f32
    ).astype(bf16)
    grad_kept, grad_came = keep_and_swap(grad_attended, 0, half_width)
    grad_first = jnp.where(half == 0, grad_kept, grad_came)
    grad_second = jnp.where(half == 0, grad_came, grad_kept)

    grad_activation = jnp.dot(cotangent_rows, down_full, preferred_element_type=f32)
    grad_hidden = gelu_pull(grad_activation)[0].astype(bf16)

    attended_heads, back_heads = attention(
        low,
        mid,
        first,
        second,
        grad_first,
        grad_second,
        start[None, :],
        cosine_full,
        sine_full,
    )
    att_kept, att_came = keep_and_swap(attended_heads, 1, half_len)
    back_kept, back_came = keep_and_swap(back_heads, 2, half_len)
    attended = in_order(att_kept, att_came, 0)
    grad_projected = in_order(back_kept, back_came, 1).reshape(3 * local_width, half_len)

    block_out = lax.dot_general(
        attended, dense_full, row_by_col, preferred_element_type=f32
    ) + lax.dot_general(activation, down_full, contract_cols, preferred_element_type=f32)
    up_grad = lax.dot_general(normed, grad_hidden, contract_rows, preferred_element_type=f32)
    down_grad = lax.dot_general(
        cotangent_rows, activation, contract_rows, preferred_element_type=f32
    )
    hidden_sum = jnp.sum(grad_hidden.astype(f32), axis=0)
    branch_own, up_part, down_part = reduce(
        sizes,
        block_out.astype(bf16),
        [up_grad.astype(bf16), down_grad.astype(bf16)],
        None,
        3,
        "reduce_first",
    )
    layer_output = (inputs + branch_own + (bias_dense + bias_down)).astype(bf16)

    block_in = lax.dot_general(
        grad_projected, projection, contract_rows_cols, preferred_element_type=f32
    ) + lax.dot_general(grad_hidden, up_full, contract_cols, preferred_element_type=f32)
    projection_grad = lax.dot_general(
        normed, grad_projected, row_by_col, preferred_element_type=f32
    )
    dense_grad = lax.dot_general(
        cotangent_rows, attended, row_by_col, preferred_element_type=f32
    )
    projected_sum = jnp.sum(grad_projected.astype(f32), axis=1)
    small = jnp.concatenate([projected_sum, hidden_sum]).reshape(-1, 128)
    grad_normed_own, projection_part, dense_part, small_total = reduce(
        sizes,
        block_in.astype(bf16),
        [projection_grad.astype(bf16), dense_grad.astype(bf16)],
        small,
        4,
        "reduce_second",
    )
    cotangent_own = cotangent[0].astype(f32)
    grad_inputs, grad_gain, grad_shift = norm_pull(grad_normed_own)
    input_grad = grad_inputs + cotangent_own
    output_sum = jnp.sum(cotangent_own, axis=0)
    sums = jnp.stack([grad_gain, grad_shift, output_sum]).reshape(3, -1, shard_rows)
    sums = jnp.pad(sums.transpose(1, 0, 2), ((0, 0), (0, 5), (0, 0)))
    totals = small_reduce(sizes, sums)
    small_flat = small_total.reshape(-1)
    return (
        layer_output[None],
        input_grad[None],
        totals[0],
        totals[1],
        projection_part.reshape(shard_rows, 3, local_width),
        small_flat[: 3 * local_width].reshape(3, local_width),
        dense_part,
        totals[2],
        up_part,
        small_flat[3 * local_width :],
        down_part,
        totals[2],
    )


contract_rows_cols = (((0,), (1,)), ((), ()))


def solution(mesh):
    placed = (
        P("fsdp", ("ctx", "tp"), None),
        P("fsdp", "ctx"),
        P("fsdp", "ctx"),
        P(("fsdp", "ctx")),
        P(("fsdp", "ctx")),
        P(("fsdp", "ctx"), None, "tp"),
        P(None, "tp"),
        P(("fsdp", "ctx"), "tp"),
        P(("fsdp", "ctx")),
        P(("fsdp", "ctx"), "tp"),
        P("tp"),
        P(("fsdp", "ctx"), "tp"),
        P(("fsdp", "ctx")),
        P("fsdp", ("ctx", "tp"), None),
    )
    return jax.shard_map(
        functools.partial(body, dict(mesh.shape)),
        mesh=mesh,
        in_specs=placed,
        out_specs=(
            P("fsdp", ("ctx", "tp"), None),
            P("fsdp", ("ctx", "tp"), None),
            P(("fsdp", "ctx")),
            P(("fsdp", "ctx")),
            P(("fsdp", "ctx"), None, "tp"),
            P(None, "tp"),
            P(("fsdp", "ctx"), "tp"),
            P(("fsdp", "ctx")),
            P(("fsdp", "ctx"), "tp"),
            P("tp"),
            P(("fsdp", "ctx"), "tp"),
            P(("fsdp", "ctx")),
        ),
        check_vma=False,
    )
```

time: 1940 us -> 762 us (0.39)
  waiting for transfers between devices: 950 us -> 32.3 us
  Pallas kernels: 0 us -> 537 us
  local copies, waits for them, and re-layouts: 416 us -> 31.8 us
  matrix products: 280 us -> 131 us
  other arithmetic: 170 us -> 24.4 us
  blocking collectives: 54.7 us -> 0 us
  loops' own time: 26 us -> 0 us
    pallas_call x0 -> x7, Pallas kernels: none -> 537 us  [the longest x2 226 us: reduce(): pl.pallas_call(kernel, out_shape=tuple(shapes), in_specs=in_specs, out_sp...]
    reduce_scatter x3 -> x0, waiting for transfers between devices: 476 us -> none  [the longest x1 285 us: body(): lax.psum_scatter(jnp.concatenate([lax.dot_general(normed, grad_projected,...]
    all_gather x6 -> x0, waiting for transfers between devices: 203 us -> none  [the longest x1 81.1 us: body(): lax.all_gather(cotangent, 'tp', axis=1, tiled=True)]
    dot_general x122 -> x10, matrix products: 256 us -> 105 us  [the longest x1 18.3 us: body(): jnp.dot(cotangent_rows, down_full, preferred_element_type=f32)]
    ppermute x5 -> x4, waiting for transfers between devices: 178 us -> 32.3 us  [keep_and_swap(): return (kept, lax.ppermute(sent, 'ctx', swap))]
    squeeze x73 -> x0, local copies, waits for them, and re-layouts: 108 us -> none  [the longest x72 105 us: body(): lax.map(attend, (query_items, key_items, value_items, prev_key_items, pre...]
    dynamic_slice x165 -> x4, local copies, waits for them, and re-layouts: 98.1 us -> 3.68 us  [the longest x2 3.59 us: keep_and_swap(): sent = lax.dynamic_slice_in_dim(values, (1 - half) * width, width, axis)]
    psum x1 -> x0, waiting for transfers between devices: 90.8 us -> none  [body(): lax.psum((grad_gain, grad_shift, output_sum, projected_full, hidden_full)...]
  transfers between devices with their start and end apart: 15 -> 4, of which waited for: 9 -> 1; matrix products, arithmetic and copies ran while one was open for 39% -> 14% of each run, Pallas kernels for 0% -> 25%
where the time goes in v1:
time: 762 us; the launch traced here: 763 us
  Pallas kernels  537 us (70%)
  matrix products  131 us (17%)
  waiting for transfers between devices  32.3 us (4%)
  local copies, waits for them, and re-layouts  31.8 us (4%)
  other arithmetic  24.4 us (3%)
    pallas_call x2, Pallas kernels, reduce(): pl.pallas_call(kernel, out_shape=tuple(shapes), in_specs=in_specs, out_sp...  226 us
    pallas_call x2, Pallas kernels, gather(): pl.pallas_call(kernel, out_shape=tuple(shapes), in_specs=[ANY] * (line_co...  181 us
    pallas_call x1, Pallas kernels, attention(): pl.pallas_call(attention_kernel, grid=(heads,), out_shape=(jax.ShapeDtype...  90.8 us
    ppermute x4, waiting for transfers between devices, keep_and_swap(): return (kept, lax.ppermute(sent, 'ctx', swap))  32.3 us
    pallas_call x1, Pallas kernels, small_reduce(): pl.pallas_call(kernel, out_shape=jax.ShapeDtypeStruct(block, f32), in_spe...  30.3 us
    dot_general x1, matrix products, body(): jnp.dot(cotangent_rows, down_full, preferred_element_type=f32)  18.3 us
    dot_general x1, matrix products, body(): lax.dot_general(cotangent_rows, activation, contract_rows, preferred_elem...  15.3 us
  transfers between devices with their start and end apart: 4, of which 1 were waited for; matrix products, arithmetic and copies ran while one was open for 14% of the time, Pallas kernels for 25%

profile of v1, /device:TPU:0, one launch (start us, length us, event | category | flops | bytes accessed | tf_op | source)
XLA Modules:
  0.0 763.1 jit_solution(13083009139148867860)
XLA Ops:
  5.3 8.4 %small_gather.1 = (f32[8,8,256]{2,1,0:T(8,128)}, s32[8,1024]{1,0:T(8,128)}) custom-call(f32[8,256]{1,0:T(8,128)} %fusion.33.block_ref, s32[8,1024]{1,0:T(8,128)} %pad.14.pair_ref), custom_call_target="tpu_custom_call" | custom-call | tf_op jit(solution)/shard_map/small_gather/pallas_call | solution.py:175
  16.8 1.6 fusion.17
  23.0 90.5 %gather_first.1 = (bf16[1024,2048]{1,0:T(8,128)(2,1)}, bf16[2048,1536]{1,0:T(8,128)(2,1)}, bf16[2048,2048]{1,0:T(8,128)(2,1)}) custom-call(bf16[256,2048]{1,0:T(8,128)(2,1)} %fusion.15.refs_0_, bf16[256,1536]{1,0:T(8,128)(2,1)} %copy.29.refs_1_, bf16[256,2048]{1,0:T(8,128)(2,1)} %refs_2_.2), custom_call_target="tpu_custom_call" | custom-call | tf_op jit(solution)/shard_map/gather_first/pallas_call | solution.py:405
  113.6 10.5 %convolution_add_fusion = f32[1536,1024]{1,0:T(8,128)S(1)} fusion(bf16[2048,1536]{1,0:T(8,128)(2,1)} %get-tuple-element.31, bf16[1024,2048]{1,0:T(8,128)(2,1)} %get-tuple-element.32, f32[1536]{0:T(1024)S(1)} %reshape.164), kind=kOutput, calls=%fused_computation.18 | convolution fusion | flops 6444023808 | bytes 16783360 | tf_op jit(solution)/shard_map/dot_general | solution.py:1091
  124.2 2.5 slice.107
  126.8 2.7 slice.128
  130.2 1.9 subtract_convert_fusion
  135.1 90.7 %gather_second.1 = (bf16[1024,2048]{1,0:T(8,128)(2,1)}, bf16[2048,512]{1,0:T(8,128)(2,1)}, bf16[2048,2048]{1,0:T(8,128)(2,1)}) custom-call(bf16[256,2048]{1,0:T(8,128)(2,1)} %bitcast.103, bf16[256,512]{1,0:T(8,128)(2,1)} %refs_1_.1, bf16[256,2048]{1,0:T(8,128)(2,1)} %refs_2_.3), custom_call_target="tpu_custom_call" | custom-call | tf_op jit(solution)/shard_map/gather_second/pallas_call | solution.py:405
  225.9 6.3 convolution_convert_fusion.4
  232.2 2.0 constant_dynamic-slice_fusion.4
  235.7 14.0 %fusion.41 = f32[1024,2048]{1,0:T(8,128)} fusion(bf16[1024,2048]{1,0:T(8,128)(2,1)S(1)} %copy-done.22, bf16[2048,2048]{1,0:T(8,128)(2,1)} %get-tuple-element.36), kind=kOutput, calls=%fused_computation.111 | convolution fusion | flops 8589934592 | bytes 20971520 | tf_op jit(solution)/shard_map/dot_general | solution.py:1108
  249.7 18.3 %convert_reduce_fusion = (f32[2048]{0:T(1024)S(1)}, bf16[1024,2048]{1,0:T(8,128)(2,1)}) fusion(f32[1024,2048]{1,0:T(8,128)} %fusion.41, f32[2048]{0:T(1024)S(1)} %convert_element_type.68, bf16[1024,2048]{1,0:T(8,128)(2,1)S(1)} %copy-done.24, bf16[2048,2048]{1,0:T(8,128)(2,1)S(1)} %bitcast.124), kind=kOutput, calls=%fused_computation.10 | convolution fusion | flops 8646555648 | bytes 25182208 | tf_op jit(solution)/shard_map/dot_general | solution.py:1119
  268.0 14.1 %fusion.38 = f32[1024,2048]{1,0:T(8,128)} fusion(bf16[2048,2048]{1,0:T(8,128)(2,1)S(1)} %bitcast.124, f32[1024,2048]{1,0:T(8,128)} %fusion.41, f32[2048]{0:T(1024)S(1)} %convert_element_type.68), kind=kOutput, calls=%fused_computation.109 | convolution fusion | flops 8610906112 | bytes 25174016 | tf_op jit(solution)/shard_map/dot_general | solution.py:1140
  282.0 15.3 %convolution_convert_fusion.1.refs_2_ = bf16[2048,2048]{1,0:T(8,128)(2,1)} fusion(bf16[1024,2048]{1,0:T(8,128)(2,1)} %get-tuple-element.34, f32[1024,2048]{1,0:T(8,128)} %fusion.41, f32[2048]{0:T(1024)S(1)} %convert_element_type.68), kind=kOutput, calls=%fused_computation.15 | convolution fusion | flops 8615100416 | bytes 20979712 | tf_op jit(solution)/shard_map/dot_general | solution.py:1142
  297.3 11.4 %convolution_convert_fusion.2.refs_1_ = bf16[2048,2048]{1,0:T(8,128)(2,1)} fusion(bf16[1024,2048]{1,0:T(8,128)(2,1)S(1)} %copy-done.22, bf16[1024,2048]{1,0:T(8,128)(2,1)S(1)} %copy-done.27), kind=kOutput, calls=%fused_computation.16 | convolution fusion | flops 8594128896 | bytes 16777216 | tf_op jit(solution)/shard_map/dot_general | solution.py:1141
  311.2 2.5 broadcast_select_fusion
  313.7 90.8 %attention.1 = (bf16[256,2048]{1,0:T(8,128)(2,1)S(1)}, bf16[3,256,2048]{2,1,0:T(8,128)(2,1)S(1)}) custom-call(s32[8]{0:T(128)S(1)} %get-tuple-element.78.low_ref, s32[8]{0:T(128)S(1)} %get-tuple-element.77.mid_ref, bf16[3,256,1024]{2,1,0:T(8,128)(2,1)S(1)} %get-tuple-element.80.first_ref, bf16[3,256,1024]{2,1,0:T(8,128)(2,1)S(1)} %get-tuple-element.79.second_ref, ...), custom_call_target="tpu_custom_call" | custom-call | flops 5368709120 | bytes 4194304 | tf_op jit(solution)/shard_map/attention/pallas_call | solution.py:962
  408.4 13.4 %fusion.42 = f32[1024,2048]{1,0:T(8,128)} fusion(bf16[1024,2048]{1,0:T(8,128)(2,1)} %get-tuple-element.76, bf16[2048,2048]{1,0:T(8,128)(2,1)S(1)} %bitcast.122), kind=kOutput, calls=%fused_computation.112 | convolution fusion | flops 8589934592 | bytes 20971520 | tf_op jit(solution)/shard_map/dot_general | solution.py:1158
  421.8 32.3 %collective-permute-done.2 = bf16[256,1024]{1,0:T(8,128)(2,1)S(1)} collective-permute-done((bf16[256,1024]{1,0:T(8,128)(2,1)S(1)}, bf16[256,1024]{1,0:T(8,128)(2,1)S(1)}, u32[]{:S(2)}, u32[]{:S(2)}) %collective-permute-start.2) | collective-permute-done | bytes 524320 | tf_op jit(solution)/shard_map/ppermute | solution.py:1102
  454.8 4.4 add_convert_fusion.1.refs_0_
  459.3 100.2 %reduce_first.1 = (f32[256,2048]{1,0:T(8,128)}, f32[256,2048]{1,0:T(8,128)}, f32[256,2048]{1,0:T(8,128)}) custom-call(bf16[1024,2048]{1,0:T(8,128)(2,1)} %add_convert_fusion.1.refs_0_, bf16[2048,2048]{1,0:T(8,128)(2,1)} %convolution_convert_fusion.2.refs_1_, bf16[2048,2048]{1,0:T(8,128)(2,1)} %convolution_convert_fusion.1.refs_2_), custom_call_target="tpu_custom_call" | custom-call | tf_op jit(solution)/shard_map/reduce_first/pallas_call | solution.py:761
  559.4 6.2 convolution_convert_fusion.3.refs_2_
  567.9 9.1 %convolution_convert_fusion.refs_1_ = bf16[2048,1536]{1,0:T(8,128)(2,1)} fusion(bf16[1024,2048]{1,0:T(8,128)(2,1)S(1)} %copy-done.23, bf16[1536,1024]{1,0:T(8,128)(2,1)S(1)} %bitcast.104), kind=kOutput, calls=%fused_computation.14 | convolution fusion | flops 6445596672 | bytes 13631488 | tf_op jit(solution)/shard_map/dot_general | solution.py:1159
  577.0 8.4 %add_convert_fusion.refs_0_ = bf16[1024,2048]{1,0:T(8,128)(2,1)} fusion(f32[1024,2048]{1,0:T(8,128)S(1)} %bitcast.130, bf16[1536,1024]{1,0:T(8,128)(2,1)S(1)} %bitcast.105, bf16[2048,1536]{1,0:T(8,128)(2,1)S(1)} %bitcast.126), kind=kOutput, calls=%fused_computation.11 | convolution fusion | flops 6446645248 | bytes 22020096 | tf_op jit(solution)/shard_map/dot_general | solution.py:1156
  586.0 125.7 %reduce_second.1 = (f32[256,2048]{1,0:T(8,128)}, f32[256,1536]{1,0:T(8,128)}, f32[256,512]{1,0:T(8,128)}, f32[28,128]{1,0:T(8,128)}) custom-call(bf16[1024,2048]{1,0:T(8,128)(2,1)} %add_convert_fusion.refs_0_, bf16[2048,1536]{1,0:T(8,128)(2,1)} %convolution_convert_fusion.refs_1_, bf16[2048,512]{1,0:T(8,128)(2,1)} %convolution_convert_fusion.3.refs_2_, ...), custom_call_target="tpu_custom_call" | custom-call | tf_op jit(solution)/shard_map/reduce_second/pallas_call | solution.py:761
  712.6 1.7 slice_bitcast_fusion
  714.4 2.1 fusion.18
  717.6 3.1 convert_reduce_fusion.2
  721.3 30.3 %small_reduce.1 = f32[8,256]{1,0:T(8,128)} custom-call(f32[8,8,256]{2,1,0:T(8,128)} %pad.17.blocks_ref), custom_call_target="tpu_custom_call" | custom-call | tf_op jit(solution)/shard_map/small_reduce/pallas_call | solution.py:816
  753.5 1.6 copy.31
  756.3 1.9 copy.37
  758.2 3.1 copy.38
  (140 shorter events, 34.3 us)
Async XLA Ops:
  0.6 21.0 %copy-start = (bf16[1,256,2048]{2,1,0:T(8,128)(2,1)S(1)}, bf16[1,256,2048]{2,1,0:T(8,128)(2,1)}, u32[]{:S(2)}) copy-start(bf16[1,256,2048]{2,1,0:T(8,128)(2,1)} %param.14) | copy-start | bytes 3145732
  0.7 20.9 %copy-start.19 = (bf16[3,512]{1,0:T(4,128)(2,1)S(1)}, bf16[3,512]{1,0:T(4,128)(2,1)}, u32[]{:S(2)}) copy-start(bf16[3,512]{1,0:T(4,128)(2,1)} %param.20) | copy-start | bytes 9220
  15.3 98.3 %copy-start.9 = (f32[8,1,256]{2,1,0:T(1,128)}, f32[8,1,256]{2,1,0:T(1,128)S(1)}, u32[]{:S(2)}) copy-start(f32[8,1,256]{2,1,0:T(1,128)S(1)} %get-tuple-element.94) | copy-start | bytes 24580
  16.8 96.8 %copy-start.11 = (f32[256]{0:T(256)}, f32[256]{0:T(256)S(1)}, u32[]{:S(2)}) copy-start(f32[256]{0:T(256)S(1)} %broadcast_multiply_fusion) | copy-start | bytes 3076
  19.0 105.1 %copy-start.15 = (f32[256]{0:T(256)}, f32[256]{0:T(256)S(1)}, u32[]{:S(2)}) copy-start(f32[256]{0:T(256)S(1)} %fusion.34) | copy-start | bytes 3076
  133.7 177.6 %collective-permute-start = (bf16[3,256,1024]{2,1,0:T(8,128)(2,1)}, bf16[3,256,1024]{2,1,0:T(8,128)(2,1)}, u32[]{:S(2)}, u32[]{:S(2)}) collective-permute-start(bf16[3,256,1024]{2,1,0:T(8,128)(2,1)} %fusion.22), channel_id=1, source_target_pairs={{0,4},{4,0},{1,5},{5,1},{2,6},{6,2},{3,7},{7,3},{8,12},{12,8},{9,1... | collective-permute-start | bytes 4718600 | tf_op jit(solution)/shard_map/ppermute | solution.py:1102
  225.9 9.8 %copy-start.22 = (bf16[1024,2048]{1,0:T(8,128)(2,1)S(1)}, bf16[1024,2048]{1,0:T(8,128)(2,1)}, u32[]{:S(2)}) copy-start(bf16[1024,2048]{1,0:T(8,128)(2,1)} %get-tuple-element.32) | copy-start | bytes 12582916
  232.2 17.5 %slice-start.2 = ((s8[8388608]{0:T(1024)(128)(4,1)}), s8[4194304]{0:T(1024)(128)(4,1)S(1)}, s32[]{:S(2)}) async-start(s8[8388608]{0:T(1024)(128)(4,1)} %bitcast.123), calls=%async_computation.2 | async-start | bytes 8388608
  234.2 75.5 %collective-permute-start.1 = (bf16[256,1024]{1,0:T(8,128)(2,1)}, bf16[256,1024]{1,0:T(8,128)(2,1)}, u32[]{:S(2)}, u32[]{:S(2)}) collective-permute-start(bf16[256,1024]{1,0:T(8,128)(2,1)} %constant_dynamic-slice_fusion.4), channel_id=1, source_target_pairs={{0,4},{4,0},{1,5},{5,1},{2,6},{6,2},{3,7},{7,3},{8,12},{12,8},{9,1... | collective-permute-start | bytes 1572872 | tf_op jit(solution)/shard_map/ppermute | solution.py:1102
  235.7 14.0 %copy-start.20 = (bf16[2048]{0:T(1024)(128)(2,1)S(1)}, bf16[2048]{0:T(1024)(128)(2,1)}, u32[]{:S(2)}) copy-start(bf16[2048]{0:T(1024)(128)(2,1)} %param.24) | copy-start | bytes 12292
  235.7 14.0 %slice-start.3 = ((s8[8388608]{0:T(1024)(128)(4,1)}), s8[4194304]{0:T(1024)(128)(4,1)S(1)}, s32[]{:S(2)}) async-start(s8[8388608]{0:T(1024)(128)(4,1)} %bitcast.123), calls=%async_computation.3 | async-start | bytes 8388608
  235.7 14.0 %copy-start.24 = (bf16[1024,2048]{1,0:T(8,128)(2,1)S(1)}, bf16[1024,2048]{1,0:T(8,128)(2,1)}, u32[]{:S(2)}) copy-start(bf16[1024,2048]{1,0:T(8,128)(2,1)} %get-tuple-element.34) | copy-start | bytes 12582916
  282.0 15.3 %copy-start.27 = (bf16[1024,2048]{1,0:T(8,128)(2,1)S(1)}, bf16[1024,2048]{1,0:T(8,128)(2,1)}, u32[]{:S(2)}) copy-start(bf16[1024,2048]{1,0:T(8,128)(2,1)} %get-tuple-element.76) | copy-start | bytes 12582916
  311.2 97.1 %slice-start = ((s8[8388608]{0:T(1024)(128)(4,1)}), s8[4194304]{0:T(1024)(128)(4,1)S(1)}, s32[]{:S(2)}) async-start(s8[8388608]{0:T(1024)(128)(4,1)} %bitcast.121), calls=%async_computation | async-start | bytes 8388608
  313.7 94.6 %slice-start.1 = ((s8[8388608]{0:T(1024)(128)(4,1)}), s8[4194304]{0:T(1024)(128)(4,1)S(1)}, s32[]{:S(2)}) async-start(s8[8388608]{0:T(1024)(128)(4,1)} %bitcast.121), calls=%async_computation.1 | async-start | bytes 8388608
  406.1 159.5 %collective-permute-start.3 = (bf16[3,256,1024]{2,1,0:T(8,128)(2,1)}, bf16[3,256,1024]{2,1,0:T(8,128)(2,1)S(1)}, u32[]{:S(2)}, u32[]{:S(2)}) collective-permute-start(bf16[3,256,1024]{2,1,0:T(8,128)(2,1)} %get-tuple-element.83), channel_id=1, source_target_pairs={{0,4},{4,0},{1,5},{5,1},{2,6},{6,2},{3,7},{7,3},{8,12},{12,8},{9,1... | collective-permute-start | bytes 4718600 | tf_op jit(solution)/shard_map/ppermute | solution.py:1102
  406.8 48.0 %slice-start.6 = ((s8[8388608]{0:T(1024)(128)(4,1)}), s8[4194304]{0:T(1024)(128)(4,1)S(1)}, s32[]{:S(2)}) async-start(s8[8388608]{0:T(1024)(128)(4,1)} %bitcast.127), calls=%async_computation.6 | async-start | bytes 8388608
  406.8 48.0 %copy-start.25 = (bf16[2048,512]{1,0:T(8,128)(2,1)S(1)}, bf16[2048,512]{1,0:T(8,128)(2,1)}, u32[]{:S(2)}) copy-start(bf16[2048,512]{1,0:T(8,128)(2,1)} %get-tuple-element.33) | copy-start | bytes 6291460
  406.8 48.0 %slice-start.7 = ((s8[8388608]{0:T(1024)(128)(4,1)}), s8[4194304]{0:T(1024)(128)(4,1)S(1)}, s32[]{:S(2)}) async-start(s8[8388608]{0:T(1024)(128)(4,1)} %bitcast.127), calls=%async_computation.7 | async-start | bytes 8388608
  406.8 47.2 %collective-permute-start.2 = (bf16[256,1024]{1,0:T(8,128)(2,1)S(1)}, bf16[256,1024]{1,0:T(8,128)(2,1)S(1)}, u32[]{:S(2)}, u32[]{:S(2)}) collective-permute-start(bf16[256,1024]{1,0:T(8,128)(2,1)S(1)} %get-tuple-element.91), channel_id=1, source_target_pairs={{0,4},{4,0},{1,5},{5,1},{2,6},{6,2},{3,7},{7,3},{8,12},{12,8},{9,1... | collective-permute-start | bytes 1572872 | tf_op jit(solution)/shard_map/ppermute | solution.py:1102
  565.7 11.3 %slice-start.4 = ((s8[6291456]{0:T(1024)(128)(4,1)}), s8[4194304]{0:T(1024)(128)(4,1)S(1)}, s32[]{:S(2)}) async-start(s8[6291456]{0:T(1024)(128)(4,1)} %bitcast.125), calls=%async_computation.4 | async-start | bytes 8388608
  565.7 11.3 %slice-start.8 = ((s8[8388608]{0:T(1024)(128)(4,1)}), s8[4194304]{0:T(1024)(128)(4,1)S(1)}, s32[]{:S(2)}) async-start(s8[8388608]{0:T(1024)(128)(4,1)} %bitcast.129), calls=%async_computation.8 | async-start | bytes 8388608
  567.9 9.1 %slice-start.5 = ((s8[6291456]{0:T(1024)(128)(4,1)}), s8[2097152]{0:T(1024)(128)(4,1)S(1)}, s32[]{:S(2)}) async-start(s8[6291456]{0:T(1024)(128)(4,1)} %bitcast.125), calls=%async_computation.5 | async-start | bytes 4194304
  567.9 9.1 %slice-start.9 = ((s8[8388608]{0:T(1024)(128)(4,1)}), s8[4194304]{0:T(1024)(128)(4,1)S(1)}, s32[]{:S(2)}) async-start(s8[8388608]{0:T(1024)(128)(4,1)} %bitcast.129), calls=%async_computation.9 | async-start | bytes 8388608
  586.0 128.4 %copy-start.1 = (bf16[1,256,2048]{2,1,0:T(8,128)(2,1)S(1)}, bf16[1,256,2048]{2,1,0:T(8,128)(2,1)}, u32[]{:S(2)}) copy-start(bf16[1,256,2048]{2,1,0:T(8,128)(2,1)} %param.14) | copy-start | bytes 3145732
  586.0 128.4 %copy-start.10 = (f32[8,1,256]{2,1,0:T(1,128)S(1)}, f32[8,1,256]{2,1,0:T(1,128)}, u32[]{:S(2)}) copy-start(f32[8,1,256]{2,1,0:T(1,128)} %copy-done.9) | copy-start | bytes 24580
  586.0 128.4 %copy-start.12 = (f32[256]{0:T(256)S(1)}, f32[256]{0:T(256)}, u32[]{:S(2)}) copy-start(f32[256]{0:T(256)} %copy-done.11) | copy-start | bytes 3076
  586.0 130.4 %copy-start.18 = (f32[256]{0:T(256)S(1)}, f32[256]{0:T(256)}, u32[]{:S(2)}) copy-start(f32[256]{0:T(256)} %copy-done.17) | copy-start | bytes 3076
  586.0 130.4 %copy-start.16 = (f32[256]{0:T(256)S(1)}, f32[256]{0:T(256)}, u32[]{:S(2)}) copy-start(f32[256]{0:T(256)} %copy-done.15) | copy-start | bytes 3076
  717.6 35.5 %copy-start.7 = (f32[256,1536]{1,0:T(8,128)S(1)}, f32[256,1536]{1,0:T(8,128)}, u32[]{:S(2)}) copy-start(f32[256,1536]{1,0:T(8,128)} %get-tuple-element.41) | copy-start | bytes 4718596
  753.0 8.3 %copy-start.21 = (f32[1,256]{1,0:T(1,128)}, f32[1,256]{1,0:T(1,128)S(1)}, u32[]{:S(2)}) copy-start(f32[1,256]{1,0:T(1,128)S(1)} %get-tuple-element.97) | copy-start | bytes 3076
  755.1 6.2 copy-start.6
  (10 other events, 33.6 us)

commit v2 on v1

--- a/solution.py
+++ b/solution.py
@@ -34,12 +34,12 @@
     return centered * lax.rsqrt(spread + epsilon) * gain_full + shift_full
 
 
-def gelu_new(values):
-    return (
-        0.5
-        * values
-        * (1.0 + jnp.tanh(root_two_over_pi * (values + 0.044715 * values * values * values)))
-    )
+def gelu_and_slope(values):
+    turned = jnp.tanh(root_two_over_pi * (values + 0.044715 * values * values * values))
+    slope = 0.5 * (1.0 + turned) + 0.5 * values * (1.0 - turned * turned) * root_two_over_pi * (
+        1.0 + 3.0 * 0.044715 * values * values
+    )
+    return 0.5 * values * (1.0 + turned), slope
 
 
 class Place:
@@ -200,11 +200,14 @@
 
         line_in, weight_in = take(line_count), take(weight_count)
         line_out, weight_out = take(line_count), take(weight_count)
-        keep, line_send, line_recv, near_send, near_recv = take(5)
-        turn_send, turn_recv, core_send, core_recv = take(4)
+        keep, near_send, near_recv, turn_send, turn_recv, core_send, core_recv = take(7)
+        line_send, line_recv = take(2) if line_count else (None, None)
         place = Place(sizes)
         up, down = place.layer < depth - 1, place.layer > 0
-        greet_line(place, plane(place))
+        if line_count:
+            greet_line(place, plane(place))
+        else:
+            greet(plane(place))
 
         def part(ref, block, rows, first=0, count=None):
             count = rows if count is None else count
@@ -409,29 +412,28 @@
         out_specs=(ANY,) * (line_count + weight_count),
         scratch_shapes=[
             DMA((line_count + weight_count,)),
-            DMA((line_count, 2, depth - 1)),
-            DMA((line_count, 2, depth - 1)),
             DMA((weight_count, chips)),
             DMA((weight_count, chips)),
             DMA((weight_count, 2, chips)),
             DMA((weight_count, 2, chips)),
             DMA((weight_count, 2 * chips)),
             DMA((weight_count, 2 * chips)),
-        ],
+        ]
+        + ([DMA((line_count, 2, depth - 1))] * 2 if line_count else []),
         compiler_params=pltpu.CompilerParams(collective_id=collective_id, has_side_effects=True),
+        cost_estimate=pl.CostEstimate(flops=0, bytes_accessed=380_000_000, transcendentals=0),
         name=name,
     )(*lines, *weights)
 
 
-def reduce(sizes, line, weights, small, collective_id, name):
-    chips, halves, depth = sizes["fsdp"] // 2, sizes["ctx"], sizes["tp"]
+def reduce(sizes, paired, rights, small, collective_id, name):
+    chips, halves = sizes["fsdp"] // 2, sizes["ctx"]
     groups = chips * halves
-    weight_count = len(weights)
-    line_rows, line_width = line.shape[0] // depth, line.shape[1]
-    block_rows = weights[0].shape[0] // (2 * groups)
-    widths = [v.shape[1] for v in weights]
+    paired_count, made_count = len(paired), len(rights)
+    weight_count = paired_count + made_count
+    block_rows = paired[0].shape[1]
+    widths = [v.shape[2] for v in paired] + [v.shape[0] for _, v in rights]
     side = block_rows // 2
-    has_small = small is not None
 
     def kernel(*refs):
         refs = list(refs)
@@ -441,20 +443,19 @@
             del refs[:count]
             return taken
 
-        (line_ref,) = take(1)
-        weight_in = take(weight_count)
-        small_ref = take(1)[0] if has_small else None
-        (line_out,) = take(1)
+        paired_in = take(paired_count)
+        factors = take(2 * made_count)
+        (small_ref,) = take(1)
         weight_out = take(weight_count)
-        small_out = take(1)[0] if has_small else None
-        flow, fresh = take(2)
-        own, pair, turn_a, turn_b, near = (take(weight_count) for _ in range(5))
-        line_send, line_recv, load_sem, core_send, core_recv = take(5)
+        (small_out,) = take(1)
+        made = take(made_count)
+        own, turn_a, turn_b, near = (take(weight_count) for _ in range(4))
+        pair = [None] * paired_count + take(made_count)
+        load_sem, core_send, core_recv = take(3)
         turn_send, turn_recv, near_send, near_recv = take(4)
-        if has_small:
-            small_pair, small_near, small_far, small_send, small_recv = take(5)
+        small_pair, small_near, small_far, small_send, small_recv = take(5)
         place = Place(sizes)
-        greet_line(place, plane(place))
+        greet(plane(place))
         pending = []
 
         def launch(copy, condition=None):
@@ -465,16 +466,22 @@
             pending.append((copy, condition))
 
         other = 1 - place.core
-        for a in range(weight_count):
+        for a in range(paired_count):
+            for number in range(groups):
+                pltpu.make_async_copy(
+                    paired_in[a].at[number], own[a].at[number], load_sem.at[a, number]
+                ).start()
+
+        def make(a):
+            at = a - paired_count
+            multiply("tt", factors[2 * at], factors[2 * at + 1], [made[at]])
             for number in range(groups):
                 chip, half = number // halves, number % halves
                 theirs = place.block(chip, other, half)
                 mine = place.block(chip, place.core, half)
                 launch(
                     send(
-                        weight_in[a].at[
-                            pl.ds(pl.multiple_of(theirs * block_rows, 16), block_rows)
-                        ],
+                        made[at].at[pl.ds(pl.multiple_of(theirs * block_rows, 16), block_rows)],
                         pair[a].at[number],
                         core_send.at[a, number],
                         core_recv.at[a, number],
@@ -482,99 +489,17 @@
                     )
                 )
                 pltpu.make_async_copy(
-                    weight_in[a].at[pl.ds(pl.multiple_of(mine * block_rows, 16), block_rows)],
+                    made[at].at[pl.ds(pl.multiple_of(mine * block_rows, 16), block_rows)],
                     own[a].at[number],
                     load_sem.at[a, number],
                 ).start()
 
-        def line_ends(way, owner):
-            step = 1 if way == 0 else -1
-            inner = (place.layer - owner) * step < 0
-            first = place.layer == (0 if way == 0 else depth - 1)
-            return step, inner, first
-
-        def line_sum(way, hop):
-            step = 1 if way == 0 else -1
-            owner = depth - 1 - hop if way == 0 else hop
-            sends = place.layer < owner if way == 0 else place.layer > owner
-            first = place.layer == (0 if way == 0 else depth - 1)
-            device = place.device(layer=jnp.clip(place.layer + step, 0, depth - 1))
-            rows = line_ref.at[pl.ds(owner * line_rows, line_rows)]
-
-            @pl.when(sends & jnp.logical_not(first))
-            def _():
-                send(
-                    rows, flow.at[way, owner], line_send.at[way, owner], line_recv.at[way, owner], device
-                ).wait_recv()
-
-                @pl.loop(0, line_rows, step=16)
-                def _(r):
-                    at = pl.ds(pl.multiple_of(r, 16), 16)
-                    start = pl.ds(pl.multiple_of(owner * line_rows + r, 16), 16)
-                    total = line_ref[start, :].astype(f32) + flow[way, owner, at, :].astype(f32)
-                    fresh[way, owner, at, :] = total.astype(bf16)
-
-                send(
-                    fresh.at[way, owner],
-                    flow.at[way, owner],
-                    line_send.at[way, owner],
-                    line_recv.at[way, owner],
-                    device,
-                ).start()
-
-            @pl.when(sends & first)
-            def _():
-                send(
-                    rows, flow.at[way, owner], line_send.at[way, owner], line_recv.at[way, owner], device
-                ).start()
-
-            pending.append(
-                (
-                    send(
-                        rows,
-                        flow.at[way, owner],
-                        line_send.at[way, owner],
-                        line_recv.at[way, owner],
-                        device,
-                    ),
-                    sends,
-                )
-            )
-
-        def line_own():
-            below, above = place.layer > 0, place.layer < depth - 1
-            mine = place.layer
-            rows = line_ref.at[pl.ds(pl.multiple_of(mine * line_rows, 16), line_rows)]
-            for way, condition in ((0, below), (1, above)):
-                pl.when(condition)(
-                    send(
-                        rows,
-                        flow.at[way, mine],
-                        line_send.at[way, mine],
-                        line_recv.at[way, mine],
-                        place.pair(),
-                    ).wait_recv
-                )
-
-            @pl.loop(0, line_rows, step=16)
-            def _(r):
-                at = pl.ds(pl.multiple_of(r, 16), 16)
-                start = pl.ds(pl.multiple_of(mine * line_rows + r, 16), 16)
-                line_out[at, :] = line_ref[start, :].astype(f32)
-
-            for way, condition in ((0, below), (1, above)):
-
-                @pl.when(condition)
-                def _(way=way):
-                    @pl.loop(0, line_rows, step=16)
-                    def _(r):
-                        at = pl.ds(pl.multiple_of(r, 16), 16)
-                        line_out[at, :] += flow[way, mine, at, :].astype(f32)
-
         def pair_sum(a, number):
             mine = own[a].at[number]
+            pltpu.make_async_copy(mine, mine, load_sem.at[a, number]).wait()
+            if a < paired_count:
+                return
             theirs = pair[a].at[number]
-            pltpu.make_async_copy(mine, mine, load_sem.at[a, number]).wait()
             send(
                 theirs, theirs, core_send.at[a, number], core_recv.at[a, number], place.pair()
             ).wait_recv()
@@ -676,67 +601,53 @@
             launch(copy)
             return copy
 
-        for way in range(2):
-            line_sum(way, 0)
-        if has_small:
-            swap_small(small_ref, small_pair, 0, place.pair())
-        for a in range(weight_count):
+        swap_small(small_ref, small_pair, 0, place.pair())
+        for a in range(paired_count):
             diagonal(a)
-        for way in range(2):
-            line_sum(way, 1)
-        for a in range(weight_count):
             direct_pairs(a)
-        if has_small:
-            send(
-                small_pair, small_pair, small_send.at[0], small_recv.at[0], place.pair()
-            ).wait_recv()
-            small_near[0] = small_ref[...] + small_pair[...]
-            for k in range(1, chips):
-                swap_small(
-                    small_near.at[0], small_near.at[k], k, place.device(chip=place.ahead(k))
-                )
-        for a in range(weight_count):
+        for a in range(paired_count, weight_count):
+            make(a)
+        send(small_pair, small_pair, small_send.at[0], small_recv.at[0], place.pair()).wait_recv()
+        small_near[0] = small_ref[...] + small_pair[...]
+        for k in range(1, chips):
+            swap_small(small_near.at[0], small_near.at[k], k, place.device(chip=place.ahead(k)))
+        for a in range(paired_count):
             direct(a)
-        for hop in range(2, depth - 1):
-            for way in range(2):
-                line_sum(way, hop)
-        if has_small:
-            total = small_near[0]
-            for k in range(1, chips):
-                piece = small_near.at[k]
-                send(piece, piece, small_send.at[k], small_recv.at[k], place.pair()).wait_recv()
-                total += small_near[k]
-            small_far[0] = total
-            swap_small(small_far.at[0], small_far.at[1], chips, place.across())
+        for a in range(paired_count, weight_count):
+            diagonal(a)
+            direct_pairs(a)
+        total = small_near[0]
+        for k in range(1, chips):
+            piece = small_near.at[k]
+            send(piece, piece, small_send.at[k], small_recv.at[k], place.pair()).wait_recv()
+            total += small_near[k]
+        small_far[0] = total
+        swap_small(small_far.at[0], small_far.at[1], chips, place.across())
         for a in range(weight_count):
             pair_sum(a, place.chip * halves + place.half)
+        for a in range(paired_count, weight_count):
+            direct(a)
         for a in range(weight_count):
             finish(a)
-        if has_small:
-            piece = small_far.at[1]
-            send(
-                piece, piece, small_send.at[chips], small_recv.at[chips], place.pair()
-            ).wait_recv()
-            small_out[...] = small_far[0] + small_far[1]
-        line_own()
+        piece = small_far.at[1]
+        send(piece, piece, small_send.at[chips], small_recv.at[chips], place.pair()).wait_recv()
+        small_out[...] = small_far[0] + small_far[1]
         for copy, condition in pending:
             if condition is None:
                 copy.wait_send()
             else:
                 pl.when(condition)(copy.wait_send)
 
-    shapes = [jax.ShapeDtypeStruct((line_rows, line_width), f32)]
-    shapes += [jax.ShapeDtypeStruct((block_rows, w), f32) for w in widths]
-    scratch = [
-        pltpu.VMEM((2, depth, line_rows, line_width), bf16),
-        pltpu.VMEM((2, depth, line_rows, line_width), bf16),
+    shapes = [jax.ShapeDtypeStruct((block_rows, w), f32) for w in widths]
+    shapes.append(jax.ShapeDtypeStruct(small.shape, f32))
+    made_shapes = [
+        jax.ShapeDtypeStruct((2 * groups * block_rows, w), bf16) for w in widths[paired_count:]
     ]
-    for rows in ((groups, block_rows), (groups, block_rows), (chips - 1, side), (chips - 1, side)):
-        scratch += [pltpu.VMEM(rows + (w,), bf16) for w in widths]
+    scratch = [pltpu.VMEM((groups, block_rows, w), bf16) for w in widths]
+    scratch += [pltpu.VMEM((chips - 1, side, w), bf16) for w in widths] * 2
     scratch += [pltpu.VMEM((chips, block_rows, w), bf16) for w in widths]
+    scratch += [pltpu.VMEM((groups, block_rows, w), bf16) for w in widths[paired_count:]]
     scratch += [
-        DMA((2, depth)),
-        DMA((2, depth)),
         DMA((weight_count, groups)),
         DMA((weight_count, groups)),
         DMA((weight_count, groups)),
@@ -744,31 +655,284 @@
         DMA((weight_count, 2, chips)),
         DMA((weight_count, chips)),
         DMA((weight_count, chips)),
+        pltpu.VMEM(small.shape, f32),
+        pltpu.VMEM((chips,) + small.shape, f32),
+        pltpu.VMEM((2,) + small.shape, f32),
+        DMA((chips + 1,)),
+        DMA((chips + 1,)),
     ]
-    arguments = [line, *weights]
-    in_specs = [VMEM] + [ANY] * weight_count
-    if has_small:
-        shapes.append(jax.ShapeDtypeStruct(small.shape, f32))
-        scratch += [
-            pltpu.VMEM(small.shape, f32),
-            pltpu.VMEM((chips,) + small.shape, f32),
-            pltpu.VMEM((2,) + small.shape, f32),
-            DMA((chips + 1,)),
-            DMA((chips + 1,)),
-        ]
-        arguments.append(small)
-        in_specs.append(VMEM)
+    factors = [v for two in rights for v in two]
     return pl.pallas_call(
         kernel,
-        out_shape=tuple(shapes),
-        in_specs=in_specs,
-        out_specs=(VMEM,) * len(shapes),
+        out_shape=tuple(shapes + made_shapes),
+        in_specs=[ANY] * (paired_count + 2 * made_count) + [VMEM],
+        out_specs=(VMEM,) * len(shapes) + (ANY,) * made_count,
         scratch_shapes=scratch,
         compiler_params=pltpu.CompilerParams(
             collective_id=collective_id, has_side_effects=True, vmem_limit_bytes=60 << 20
         ),
+        cost_estimate=pl.CostEstimate(flops=0, bytes_accessed=400_000_000, transcendentals=0),
         name=name,
-    )(*arguments)
+    )(*paired, *factors, small)[: weight_count + 1]
+
+
+def multiply(kind, left, right, outs, finish=None, extra=(), tile=512):
+    dims = (((0 if kind[0] == "t" else 1,), (1 if kind[1] == "t" else 0,)), ((), ()))
+    rows = left.shape[1] if kind[0] == "t" else left.shape[0]
+    width = right.shape[0] if kind[1] == "t" else right.shape[1]
+    depth = right.shape[1] if kind[1] == "t" else right.shape[0]
+    tile = min(tile, width)
+    right_spec = (
+        pl.BlockSpec((tile, depth), lambda n: (n, 0))
+        if kind[1] == "t"
+        else pl.BlockSpec((depth, tile), lambda n: (0, n))
+    )
+    out_spec = pl.BlockSpec((rows, tile), lambda n: (0, n))
+    extra_specs = [pl.BlockSpec((v.shape[0], tile), lambda n: (0, n)) for v in extra]
+
+    def step(left_ref, right_ref, *rest):
+        found = lax.dot_general(left_ref[...], right_ref[...], dims, preferred_element_type=f32)
+        results = (found,)
+        if finish is not None:
+            results = finish(found, *(v[...] for v in rest[: len(extra)]))
+        for ref, value in zip(rest[len(extra) :], results):
+            ref[...] = value.astype(ref.dtype)
+
+    pltpu.emit_pipeline(
+        step,
+        grid=(width // tile,),
+        in_specs=[pl.BlockSpec(left.shape, lambda n: (0, 0)), right_spec, *extra_specs],
+        out_specs=[out_spec] * len(outs),
+    )(left, right, *extra, *outs)
+
+
+def half_rows(ref, half, count):
+    return ref.at[pl.ds(pl.multiple_of(half * count, count), count)]
+
+
+def exchange_forward(sizes, triple, normed, up_full, up_bias, down_full):
+    kinds, width, length = triple.shape
+    count = width // 2
+    rows, hidden = normed.shape[0], up_full.shape[1]
+
+    def kernel(triple_ref, normed_ref, up_ref, bias_ref, down_ref, *rest):
+        both, activation, slope, feed, sems = rest
+        place = Place(sizes)
+        greet([place.across()])
+
+        def heads(half):
+            return triple_ref.at[:, pl.ds(pl.multiple_of(half * count, count), count)]
+
+        keep = pltpu.make_async_copy(heads(place.half), both.at[place.half], sems.at[0])
+        away = send(
+            heads(1 - place.half), both.at[place.half], sems.at[1], sems.at[2], place.across()
+        )
+        away.start()
+        keep.start()
+
+        def gelu(found, bias):
+            return gelu_and_slope(found + bias)
+
+        multiply("nn", normed_ref, up_ref, [activation, slope], gelu, [bias_ref])
+        multiply("nt", activation, down_ref, [feed])
+        keep.wait()
+        away.wait_send()
+        came = both.at[1 - place.half]
+        send(came, came, sems.at[1], sems.at[2], place.across()).wait_recv()
+
+    return pl.pallas_call(
+        kernel,
+        out_shape=(
+            jax.ShapeDtypeStruct((2, kinds, count, length), bf16),
+            jax.ShapeDtypeStruct((rows, hidden), bf16),
+            jax.ShapeDtypeStruct((rows, hidden), bf16),
+            jax.ShapeDtypeStruct((rows, down_full.shape[0]), f32),
+        ),
+        in_specs=[ANY] * 5,
+        out_specs=(ANY,) * 4,
+        scratch_shapes=[DMA((3,))],
+        compiler_params=pltpu.CompilerParams(
+            collective_id=4, has_side_effects=True, vmem_limit_bytes=60 << 20
+        ),
+        cost_estimate=pl.CostEstimate(flops=0, bytes_accessed=130_000_000, transcendentals=0),
+        name="exchange_forward",
+    )(triple, normed, up_full, up_bias, down_full)
+
+
+def exchange_middle(sizes, attended, grad_attended, cotangent, down_full, slope):
+    width, total = attended.shape
+    length = total // 2
+    rows, hidden = slope.shape
+
+    def kernel(attended_ref, grad_ref, cotangent_ref, down_ref, slope_ref, *rest):
+        full, both, grad_hidden, sems = rest
+        place = Place(sizes)
+        greet([place.across()])
+        here, there = place.half, 1 - place.half
+
+        def tokens(half):
+            return attended_ref.at[:, pl.ds(pl.multiple_of(half * length, length), length)]
+
+        copies = [
+            send(
+                tokens(there), half_rows(full, here, width), sems.at[0], sems.at[1], place.across()
+            ),
+            send(
+                half_rows(grad_ref, there, width),
+                both.at[here],
+                sems.at[2],
+                sems.at[3],
+                place.across(),
+            ),
+        ]
+        kept = [
+            pltpu.make_async_copy(tokens(here), half_rows(full, here, width), sems.at[4]),
+            pltpu.make_async_copy(half_rows(grad_ref, here, width), both.at[here], sems.at[5]),
+        ]
+        for copy in copies + kept:
+            copy.start()
+        multiply(
+            "nn",
+            cotangent_ref,
+            down_ref,
+            [grad_hidden],
+            lambda found, slope: (found * slope.astype(f32),),
+            [slope_ref],
+        )
+        for copy in kept:
+            copy.wait()
+        for number, came in enumerate((half_rows(full, there, width), both.at[there])):
+            copies[number].wait_send()
+            send(
+                came, came, sems.at[2 * number], sems.at[2 * number + 1], place.across()
+            ).wait_recv()
+
+    return pl.pallas_call(
+        kernel,
+        out_shape=(
+            jax.ShapeDtypeStruct((2 * width, length), bf16),
+            jax.ShapeDtypeStruct((2, width, length), bf16),
+            jax.ShapeDtypeStruct((rows, hidden), bf16),
+        ),
+        in_specs=[ANY] * 5,
+        out_specs=(ANY,) * 3,
+        scratch_shapes=[DMA((6,))],
+        compiler_params=pltpu.CompilerParams(
+            collective_id=5, has_side_effects=True, vmem_limit_bytes=60 << 20
+        ),
+        cost_estimate=pl.CostEstimate(flops=0, bytes_accessed=90_000_000, transcendentals=0),
+        name="exchange_middle",
+    )(attended, grad_attended, cotangent, down_full, slope)
+
+
+def exchange_back(
+    sizes, back, normed, grad_hidden, cotangent, activation, up_full, projection
+):
+    kinds, width, total = back.shape
+    length = total // 2
+    chips, halves = sizes["fsdp"] // 2, sizes["ctx"]
+    rows, model = normed.shape
+    hidden = grad_hidden.shape[1]
+    span = model // (2 * chips)
+
+    def kernel(
+        back_ref, normed_ref, hidden_ref, cotangent_ref, activation_ref, up_ref, weight_ref, *rest
+    ):
+        full, up_sum, down_sum, block_in, up_made, down_made, up_came, down_came, feed = rest[:9]
+        sems, core_send, core_recv = rest[9:]
+        place = Place(sizes)
+        greet([place.across(), place.pair()])
+        here, there = place.half, 1 - place.half
+        other = 1 - place.core
+
+        def tokens(half):
+            return back_ref.at[:, :, pl.ds(pl.multiple_of(half * length, length), length)]
+
+        def heads(half):
+            return full.at[:, pl.ds(pl.multiple_of(half * width, width), width)]
+
+        away = send(tokens(there), heads(here), sems.at[0], sems.at[1], place.across())
+        keep = pltpu.make_async_copy(tokens(here), heads(here), sems.at[2])
+        away.start()
+        keep.start()
+
+        def to_pair(number, made, came):
+            copies = []
+            for chip in range(chips):
+                copies.append(
+                    send(
+                        made.at[pl.ds(pl.multiple_of((2 * chip + other) * span, 16), span)],
+                        came.at[pl.ds(chip * span, span)],
+                        core_send.at[number, chip],
+                        core_recv.at[number, chip],
+                        place.pair(),
+                    )
+                )
+                copies[-1].start()
+            return copies
+
+        def add_pair(copies, made, came, out):
+            for copy in copies:
+                copy.wait()
+
+            def step(mine, theirs, out_ref):
+                out_ref[...] = (mine[...].astype(f32) + theirs[...].astype(f32)).astype(bf16)
+
+            wide = hidden // 2
+            pltpu.emit_pipeline(
+                step,
+                grid=(chips, 2),
+                in_specs=[
+                    pl.BlockSpec((span, wide), lambda i, j: (2 * i + place.core, j)),
+                    pl.BlockSpec((span, wide), lambda i, j: (i, j)),
+                ],
+                out_specs=[pl.BlockSpec((span, wide), lambda i, j: (i, j))],
+            )(made, came, out)
+
+        multiply("tn", normed_ref, hidden_ref, [up_made])
+        up_copies = to_pair(0, up_made, up_came)
+        multiply("tn", cotangent_ref, activation_ref, [down_made])
+        down_copies = to_pair(1, down_made, down_came)
+        multiply("nt", hidden_ref, up_ref, [feed])
+        add_pair(up_copies, up_made, up_came, up_sum)
+        add_pair(down_copies, down_made, down_came, down_sum)
+        keep.wait()
+        away.wait_send()
+        send(heads(there), heads(there), sems.at[0], sems.at[1], place.across()).wait_recv()
+        multiply(
+            "tt",
+            full.reshape(2 * kinds * width, length),
+            weight_ref,
+            [block_in],
+            lambda found, before: (found + before,),
+            [feed],
+        )
+
+    product = jax.ShapeDtypeStruct((model, hidden), bf16)
+    part = jax.ShapeDtypeStruct((model // 2, hidden), bf16)
+    results = pl.pallas_call(
+        kernel,
+        out_shape=(
+            jax.ShapeDtypeStruct((kinds, 2 * width, length), bf16),
+            part,
+            part,
+            jax.ShapeDtypeStruct((rows, model), bf16),
+            product,
+            product,
+            part,
+            part,
+            jax.ShapeDtypeStruct((rows, model), f32),
+        ),
+        in_specs=[ANY] * 7,
+        out_specs=(ANY,) * 9,
+        scratch_shapes=[DMA((3,)), DMA((2, chips)), DMA((2, chips))],
+        compiler_params=pltpu.CompilerParams(
+            collective_id=6, has_side_effects=True, vmem_limit_bytes=60 << 20
+        ),
+        cost_estimate=pl.CostEstimate(flops=0, bytes_accessed=220_000_000, transcendentals=0),
+        name="exchange_back",
+    )(back, normed, grad_hidden, cotangent, activation, up_full, projection)
+    return results[:4]
 
 
 def small_reduce(sizes, blocks):
@@ -826,179 +990,254 @@
             DMA((depth - 1,)),
             DMA((depth - 1,)),
         ],
-        compiler_params=pltpu.CompilerParams(collective_id=5, has_side_effects=True),
+        compiler_params=pltpu.CompilerParams(collective_id=3, has_side_effects=True),
         name="small_reduce",
     )(blocks)
 
 
-def attention_kernel(
+def tile_at(number):
+    return pl.ds(pl.multiple_of(number * TILE, TILE), TILE)
+
+
+def allowed(kb, j, start):
+    places = kb * TILE + lax.broadcasted_iota(jnp.int32, (TILE, TILE), 0)
+    own = j * TILE + lax.broadcasted_iota(jnp.int32, (TILE, TILE), 1)
+    return (places >= start) & (places <= own)
+
+
+def attend_kernel(
     low_ref,
     mid_ref,
-    first_ref,
-    second_ref,
-    grad_first_ref,
-    grad_second_ref,
+    triple_ref,
+    start_ref,
+    attended_ref,
+    log_ref,
+    query_t,
+    key_t,
+    value_t,
+    key_rows,
+    scores,
+):
+    length = triple_ref.shape[3]
+    heads = triple_ref.shape[2] // HD
+    score_scale = 1.0 / math.sqrt(HD)
+    for number, ref in enumerate((query_t, key_t, value_t)):
+        for part in range(2):
+            piece = triple_ref[part, number]
+            ref[:, part * length : (part + 1) * length] = (
+                piece * score_scale if number == 0 else piece
+            )
+    rows = [slice(h * HD, (h + 1) * HD) for h in range(heads)]
+    for h in range(heads):
+        key_rows[h] = key_t[rows[h], :].T
+
+    @pl.loop(0, 2 * length // TILE)
+    def _(j):
+        here = tile_at(j)
+        start = start_ref[:, here]
+        low, mid = low_ref[j], mid_ref[j]
+        queries = [query_t[row, here] for row in rows]
+
+        def score_with(masked):
+            def score(kb, highest):
+                ok = allowed(kb, j, start) if masked else None
+                raised = []
+                for h in range(heads):
+                    found = jnp.dot(
+                        key_rows[h, tile_at(kb), :], queries[h], preferred_element_type=f32
+                    )
+                    if masked:
+                        found = jnp.where(ok, found, big_negative)
+                    scores[h, tile_at(kb), :] = found
+                    raised.append(
+                        jnp.maximum(highest[h], jnp.max(found, axis=0, keepdims=True))
+                    )
+                return tuple(raised)
+
+            return score
+
+        highest = tuple(jnp.full((1, TILE), big_negative, f32) for _ in range(heads))
+        highest = lax.fori_loop(low, mid, score_with(True), highest)
+        highest = lax.fori_loop(mid, j, score_with(False), highest)
+        highest = score_with(True)(j, highest)
+
+        def weigh(kb, carry):
+            after = []
+            for h in range(heads):
+                total, mixed = carry[h]
+                prob = jnp.exp(scores[h, tile_at(kb), :] - highest[h])
+                total = total + jnp.sum(prob, axis=0, keepdims=True)
+                mixed = mixed + jnp.dot(
+                    value_t[rows[h], tile_at(kb)], prob.astype(bf16), preferred_element_type=f32
+                )
+                after.append((total, mixed))
+            return tuple(after)
+
+        empty = tuple(
+            (jnp.zeros((1, TILE), f32), jnp.zeros((HD, TILE), f32)) for _ in range(heads)
+        )
+        result = lax.fori_loop(low, j + 1, weigh, empty)
+        for h in range(heads):
+            total, mixed = result[h]
+            attended_ref[rows[h], here] = (mixed / total).astype(bf16)
+            log_ref[h, :, here] = highest[h] + jnp.log(total)
+
+
+def turned_back(values, cosine, sine):
+    half_rot = ROT // 2
+    leading = values[:half_rot]
+    trailing = values[half_rot:ROT]
+    return jnp.concatenate(
+        [
+            leading * cosine + trailing * sine,
+            trailing * cosine - leading * sine,
+            values[ROT:],
+        ],
+        axis=0,
+    )
+
+
+def attend_back_kernel(
+    low_ref,
+    mid_ref,
+    triple_ref,
+    grad_ref,
+    attended_ref,
+    log_ref,
     start_ref,
     cosine_ref,
     sine_ref,
-    attended_ref,
     back_ref,
     query_t,
     key_t,
-    value_t,
     grad_t,
     key_rows,
     value_rows,
-    scores,
-    probs,
     key_sum,
     value_sum,
 ):
-    length = first_ref.shape[2]
-    total_length = 2 * length
+    length = triple_ref.shape[3]
+    heads = triple_ref.shape[2] // HD
     score_scale = 1.0 / math.sqrt(HD)
-    for number, ref in enumerate((query_t, key_t, value_t)):
-        scale = score_scale if number == 0 else 1.0
-        for part, source in enumerate((first_ref, second_ref)):
-            piece = source[number]
-            ref[:, part * length : (part + 1) * length] = piece * scale if number == 0 else piece
-    grad_t[:, :length] = grad_first_ref[...]
-    grad_t[:, length:] = grad_second_ref[...]
-    key_rows[...] = key_t[...].T
-    value_rows[...] = value_t[...].T
+    rows = [slice(h * HD, (h + 1) * HD) for h in range(heads)]
+    for part in range(2):
+        span = slice(part * length, (part + 1) * length)
+        query_t[:, span] = triple_ref[part, 0] * score_scale
+        key_t[:, span] = triple_ref[part, 1]
+        grad_t[:, span] = grad_ref[part]
+        for h in range(heads):
+            value_rows[h, span, :] = triple_ref[part, 2, rows[h]].T
+    for h in range(heads):
+        key_rows[h] = key_t[rows[h], :].T
     key_sum[...] = jnp.zeros_like(key_sum)
     value_sum[...] = jnp.zeros_like(value_sum)
 
-    def turned_back(values, cosine, sine):
-        half_rot = ROT // 2
-        leading = values[:half_rot]
-        trailing = values[half_rot:ROT]
-        return jnp.concatenate(
-            [
-                leading * cosine + trailing * sine,
-                trailing * cosine - leading * sine,
-                values[ROT:],
-            ],
-            axis=0,
-        )
-
-    @pl.loop(0, total_length // TILE)
+    @pl.loop(0, 2 * length // TILE)
     def _(j):
-        here = pl.ds(pl.multiple_of(j * TILE, TILE), TILE)
-        query = query_t[:, here]
-        grad = grad_t[:, here]
+        here = tile_at(j)
         start = start_ref[:, here]
         low, mid = low_ref[j], mid_ref[j]
-
-        def at(kb):
-            return pl.ds(pl.multiple_of(kb * TILE, TILE), TILE)
-
-        def plain(kb, highest):
-            found = jnp.dot(key_rows[at(kb), :], query, preferred_element_type=f32)
-            scores[at(kb), :] = found
-            return jnp.maximum(highest, jnp.max(found, axis=0, keepdims=True))
-
-        def masked(kb, highest):
-            found = jnp.dot(key_rows[at(kb), :], query, preferred_element_type=f32)
-            places = kb * TILE + lax.broadcasted_iota(jnp.int32, (TILE, TILE), 0)
-            own = j * TILE + lax.broadcasted_iota(jnp.int32, (TILE, TILE), 1)
-            found = jnp.where((places >= start) & (places <= own), found, big_negative)
-            scores[at(kb), :] = found
-            return jnp.maximum(highest, jnp.max(found, axis=0, keepdims=True))
-
-        highest = jnp.full((1, TILE), big_negative, f32)
-        highest = lax.fori_loop(low, mid, masked, highest)
-        highest = lax.fori_loop(mid, j, plain, highest)
-        highest = masked(j, highest)
-
-        def weigh(kb, carry):
-            total, mixed = carry
-            prob = jnp.exp(scores[at(kb), :] - highest)
-            total = total + jnp.sum(prob, axis=0, keepdims=True)
-            prob = prob.astype(bf16)
-            probs[at(kb), :] = prob
-            mixed = mixed + jnp.dot(value_t[:, at(kb)], prob, preferred_element_type=f32)
-            return total, mixed
-
-        total, mixed = lax.fori_loop(
-            low, j + 1, weigh, (jnp.zeros((1, TILE), f32), jnp.zeros((HD, TILE), f32))
-        )
-        over = 1.0 / total
-        mixed = mixed * over
-        attended_ref[:, here] = mixed.astype(bf16)
-        grad_wide = grad.astype(f32)
-        delta = jnp.sum(grad_wide * mixed, axis=0, keepdims=True)
-        query_over = (query.astype(f32) * over).T.astype(bf16)
-        grad_over = (grad_wide * over).T.astype(bf16)
-
-        def pull(kb, query_back):
-            prob = probs[at(kb), :]
-            down = jnp.dot(value_rows[at(kb), :], grad, preferred_element_type=f32)
-            score_back = (prob.astype(f32) * (down - delta)).astype(bf16)
-            value_sum[at(kb), :] += jnp.dot(prob, grad_over, preferred_element_type=f32)
-            key_sum[at(kb), :] += jnp.dot(score_back, query_over, preferred_element_type=f32)
-            return query_back + jnp.dot(
-                key_t[:, at(kb)], score_back, preferred_element_type=f32
+        queries = [query_t[row, here] for row in rows]
+        grads = [grad_t[row, here] for row in rows]
+        query_rows = [value.T for value in queries]
+        grad_rows = [value.T for value in grads]
+        logs = [log_ref[h, :, here] for h in range(heads)]
+        deltas = [
+            jnp.sum(
+                grads[h].astype(f32) * attended_ref[rows[h], here].astype(f32),
+                axis=0,
+                keepdims=True,
             )
-
-        query_back = lax.fori_loop(low, j + 1, pull, jnp.zeros((HD, TILE), f32))
-        query_back = query_back * (over * score_scale)
-        back_ref[0, :, here] = turned_back(
-            query_back, cosine_ref[:, here], sine_ref[:, here]
+            for h in range(heads)
+        ]
+
+        def pull_with(masked):
+            def pull(kb, query_back):
+                ok = allowed(kb, j, start) if masked else None
+                after = []
+                for h in range(heads):
+                    score = jnp.dot(
+                        key_rows[h, tile_at(kb), :], queries[h], preferred_element_type=f32
+                    )
+                    if masked:
+                        score = jnp.where(ok, score, big_negative)
+                    prob = jnp.exp(score - logs[h])
+                    down = jnp.dot(
+                        value_rows[h, tile_at(kb), :], grads[h], preferred_element_type=f32
+                    )
+                    score_back = (prob * (down - deltas[h])).astype(bf16)
+                    value_sum[h, tile_at(kb), :] += jnp.dot(
+                        prob.astype(bf16), grad_rows[h], preferred_element_type=f32
+                    )
+                    key_sum[h, tile_at(kb), :] += jnp.dot(
+                        score_back, query_rows[h], preferred_element_type=f32
+                    )
+                    after.append(
+                        query_back[h]
+                        + jnp.dot(
+                            key_t[rows[h], tile_at(kb)], score_back, preferred_element_type=f32
+                        )
+                    )
+                return tuple(after)
+
+            return pull
+
+        query_back = tuple(jnp.zeros((HD, TILE), f32) for _ in range(heads))
+        query_back = lax.fori_loop(low, mid, pull_with(True), query_back)
+        query_back = lax.fori_loop(mid, j, pull_with(False), query_back)
+        query_back = pull_with(True)(j, query_back)
+        for h in range(heads):
+            back_ref[0, rows[h], here] = turned_back(
+                query_back[h] * score_scale, cosine_ref[:, here], sine_ref[:, here]
+            ).astype(bf16)
+
+    for h in range(heads):
+        back_ref[1, rows[h], :] = turned_back(
+            key_sum[h].T, cosine_ref[...], sine_ref[...]
         ).astype(bf16)
-
-    back_ref[1] = turned_back(key_sum[...].T, cosine_ref[...], sine_ref[...]).astype(bf16)
-    back_ref[2] = value_sum[...].T.astype(bf16)
-
-
-def attention(low, mid, first, second, grad_first, grad_second, start, cosine, sine):
-    width, length = first.shape[1], first.shape[2]
-    total = 2 * length
-    heads = width // HD
-    spec = pl.BlockSpec((3, HD, length), lambda h: (0, h, 0))
-    grad_spec = pl.BlockSpec((HD, length), lambda h: (h, 0))
-    whole = lambda rows: pl.BlockSpec((rows, total), lambda h: (0, 0))
-    area = total * total // 2 * heads
+        back_ref[2, rows[h], :] = value_sum[h].T.astype(bf16)
+
+
+def attend(low, mid, triple, start):
+    width, length = triple.shape[2], triple.shape[3]
+    total, heads = 2 * length, width // HD
+    area = total * total // 3 * heads
     return pl.pallas_call(
-        attention_kernel,
-        grid=(heads,),
+        attend_kernel,
         out_shape=(
             jax.ShapeDtypeStruct((width, total), bf16),
-            jax.ShapeDtypeStruct((3, width, total), bf16),
+            jax.ShapeDtypeStruct((heads, 1, total), f32),
         ),
-        in_specs=[
-            SMEM,
-            SMEM,
-            spec,
-            spec,
-            grad_spec,
-            grad_spec,
-            whole(1),
-            whole(ROT // 2),
-            whole(ROT // 2),
-        ],
-        out_specs=(
-            pl.BlockSpec((HD, total), lambda h: (h, 0)),
-            pl.BlockSpec((3, HD, total), lambda h: (0, h, 0)),
+        in_specs=[SMEM, SMEM, VMEM, VMEM],
+        out_specs=(VMEM, VMEM),
+        scratch_shapes=[pltpu.VMEM((width, total), bf16)] * 3
+        + [pltpu.VMEM((heads, total, HD), bf16), pltpu.VMEM((heads, total, TILE), f32)],
+        compiler_params=pltpu.CompilerParams(vmem_limit_bytes=48 << 20),
+        cost_estimate=pl.CostEstimate(
+            flops=50 * area * HD, bytes_accessed=8 * width * total, transcendentals=area
         ),
-        scratch_shapes=[
-            pltpu.VMEM((HD, total), bf16),
-            pltpu.VMEM((HD, total), bf16),
-            pltpu.VMEM((HD, total), bf16),
-            pltpu.VMEM((HD, total), bf16),
-            pltpu.VMEM((total, HD), bf16),
-            pltpu.VMEM((total, HD), bf16),
-            pltpu.VMEM((total, TILE), f32),
-            pltpu.VMEM((total, TILE), bf16),
-            pltpu.VMEM((total, HD), f32),
-            pltpu.VMEM((total, HD), f32),
-        ],
-        compiler_params=pltpu.CompilerParams(vmem_limit_bytes=40 << 20),
+        name="attend",
+    )(low, mid, triple, start)
+
+
+def attend_back(low, mid, triple, grad, attended, log_sum, start, cosine, sine):
+    width, length = triple.shape[2], triple.shape[3]
+    total, heads = 2 * length, width // HD
+    area = total * total // 3 * heads
+    return pl.pallas_call(
+        attend_back_kernel,
+        out_shape=jax.ShapeDtypeStruct((3, width, total), bf16),
+        in_specs=[SMEM, SMEM] + [VMEM] * 7,
+        out_specs=VMEM,
+        scratch_shapes=[pltpu.VMEM((width, total), bf16)] * 3
+        + [pltpu.VMEM((heads, total, HD), bf16)] * 2
+        + [pltpu.VMEM((heads, total, HD), f32)] * 2,
+        compiler_params=pltpu.CompilerParams(vmem_limit_bytes=48 << 20),
         cost_estimate=pl.CostEstimate(
-            flops=10 * area * HD, bytes_accessed=8 * width * total, transcendentals=area
+            flops=100 * area * HD, bytes_accessed=12 * width * total, transcendentals=area
         ),
-        name="attention",
-    )(low, mid, first, second, grad_first, grad_second, start, cosine, sine)
+        name="attend_back",
+    )(low, mid, triple, grad, attended, log_sum, start, cosine, sine)
 
 
 def rotate_rows(values, cosine, sine):
@@ -1013,6 +1252,10 @@
         ],
         axis=1,
     )
+
+
+def ordered(*values):
+    return lax.optimization_barrier(values)
 
 
 def body(
@@ -1037,10 +1280,8 @@
     local_width = projection_weight.shape[2]
     hidden_width = up_weight.shape[1]
     shard_rows = norm_gain.shape[0]
-    half_width = local_width // 2
     half = lax.axis_index("ctx")
     total_len = 2 * half_len
-    swap = [(0, 1), (1, 0)]
 
     vectors = jnp.stack([norm_gain, norm_bias, dense_bias, down_bias]).astype(f32)
     vectors = jnp.pad(vectors, ((0, 4), (0, 0)))
@@ -1078,16 +1319,20 @@
 
     inputs = tokens[0].astype(f32)
     normed_values, norm_pull = jax.vjp(layer_norm, inputs, gain_full, shift_full)
-    normed, projection, up_full = gather(
+    normed = lax.all_gather(normed_values.astype(bf16), "tp", axis=0, tiled=True)
+    projection, up_full, dense_full, down_full = gather(
         sizes,
-        [normed_values.astype(bf16)],
-        [projection_weight.reshape(shard_rows, 3 * local_width), up_weight],
+        [],
+        [
+            projection_weight.reshape(shard_rows, 3 * local_width),
+            up_weight,
+            dense_weight,
+            down_weight,
+        ],
         1,
-        "gather_first",
-    )
-    cotangent_rows, dense_full, down_full = gather(
-        sizes, [cotangent[0]], [dense_weight, down_weight], 2, "gather_second"
-    )
+        "gather_weights",
+    )
+    cotangent_rows = lax.all_gather(cotangent[0], "tp", axis=0, tiled=True)
     projected = lax.dot_general(projection, normed, row_by_col, preferred_element_type=f32)
     projected = projected + projection_bias.astype(f32).reshape(3 * local_width)[:, None]
     projected = projected.reshape(3, local_width, half_len)
@@ -1095,83 +1340,52 @@
         projected[:2].reshape(2 * local_width // HD, HD, half_len), cosine_own, sine_own
     ).reshape(2, local_width, half_len)
     triple = jnp.concatenate([turned, projected[2:]], axis=0).astype(bf16)
-
-    def keep_and_swap(values, axis, width):
-        kept = lax.dynamic_slice_in_dim(values, half * width, width, axis)
-        sent = lax.dynamic_slice_in_dim(values, (1 - half) * width, width, axis)
-        return kept, lax.ppermute(sent, "ctx", swap)
-
-    kept, came = keep_and_swap(triple, 1, half_width)
-    first = jnp.where(half == 0, kept, came)
-    second = jnp.where(half == 0, came, kept)
-
-    hidden_pre = jnp.dot(normed, up_full, preferred_element_type=f32) + up_bias.astype(f32)
-    gelu_values, gelu_pull = jax.vjp(gelu_new, hidden_pre)
-    activation = gelu_values.astype(bf16)
-
+    both, activation, slope, feed_out = exchange_forward(
+        sizes, triple, normed, up_full, up_bias.astype(f32)[None, :], down_full
+    )
+    attended_heads, log_sum = attend(low, mid, both, start[None, :])
+    cotangent_rows, log_sum = ordered(cotangent_rows, log_sum)
     grad_attended = lax.dot_general(
         dense_full, cotangent_rows, row_by_col, preferred_element_type=f32
     ).astype(bf16)
-    grad_kept, grad_came = keep_and_swap(grad_attended, 0, half_width)
-    grad_first = jnp.where(half == 0, grad_kept, grad_came)
-    grad_second = jnp.where(half == 0, grad_came, grad_kept)
-
-    grad_activation = jnp.dot(cotangent_rows, down_full, preferred_element_type=f32)
-    grad_hidden = gelu_pull(grad_activation)[0].astype(bf16)
-
-    attended_heads, back_heads = attention(
+    attended, grad_both, grad_hidden = exchange_middle(
+        sizes, attended_heads, grad_attended, cotangent_rows, down_full, slope
+    )
+    block_out = (
+        lax.dot_general(attended, dense_full, row_by_col, preferred_element_type=f32) + feed_out
+    ).astype(bf16)
+    branch_own = lax.psum_scatter(block_out, "tp", scatter_dimension=0, tiled=True)
+    grad_both, block_out = ordered(grad_both, block_out)
+    back_heads = attend_back(
         low,
         mid,
-        first,
-        second,
-        grad_first,
-        grad_second,
+        both,
+        grad_both,
+        attended_heads,
+        log_sum,
         start[None, :],
         cosine_full,
         sine_full,
     )
-    att_kept, att_came = keep_and_swap(attended_heads, 1, half_len)
-    back_kept, back_came = keep_and_swap(back_heads, 2, half_len)
-    attended = in_order(att_kept, att_came, 0)
-    grad_projected = in_order(back_kept, back_came, 1).reshape(3 * local_width, half_len)
-
-    block_out = lax.dot_general(
-        attended, dense_full, row_by_col, preferred_element_type=f32
-    ) + lax.dot_general(activation, down_full, contract_cols, preferred_element_type=f32)
-    up_grad = lax.dot_general(normed, grad_hidden, contract_rows, preferred_element_type=f32)
-    down_grad = lax.dot_general(
-        cotangent_rows, activation, contract_rows, preferred_element_type=f32
-    )
+    grad_projected, up_sum, down_sum, block_in = exchange_back(
+        sizes, back_heads, normed, grad_hidden, cotangent_rows, activation, up_full, projection
+    )
+    grad_projected = grad_projected.reshape(3 * local_width, half_len)
+    block_in, branch_own = ordered(block_in, branch_own)
+    grad_normed_own = lax.psum_scatter(block_in, "tp", scatter_dimension=0, tiled=True).astype(f32)
     hidden_sum = jnp.sum(grad_hidden.astype(f32), axis=0)
-    branch_own, up_part, down_part = reduce(
-        sizes,
-        block_out.astype(bf16),
-        [up_grad.astype(bf16), down_grad.astype(bf16)],
-        None,
-        3,
-        "reduce_first",
-    )
-    layer_output = (inputs + branch_own + (bias_dense + bias_down)).astype(bf16)
-
-    block_in = lax.dot_general(
-        grad_projected, projection, contract_rows_cols, preferred_element_type=f32
-    ) + lax.dot_general(grad_hidden, up_full, contract_cols, preferred_element_type=f32)
-    projection_grad = lax.dot_general(
-        normed, grad_projected, row_by_col, preferred_element_type=f32
-    )
-    dense_grad = lax.dot_general(
-        cotangent_rows, attended, row_by_col, preferred_element_type=f32
-    )
     projected_sum = jnp.sum(grad_projected.astype(f32), axis=1)
     small = jnp.concatenate([projected_sum, hidden_sum]).reshape(-1, 128)
-    grad_normed_own, projection_part, dense_part, small_total = reduce(
+    groups = sizes["fsdp"] // 2 * sizes["ctx"]
+    up_part, down_part, projection_part, dense_part, small_total = reduce(
         sizes,
-        block_in.astype(bf16),
-        [projection_grad.astype(bf16), dense_grad.astype(bf16)],
+        [v.reshape(groups, shard_rows, hidden_width) for v in (up_sum, down_sum)],
+        [(normed, grad_projected), (cotangent_rows, attended)],
         small,
-        4,
-        "reduce_second",
-    )
+        2,
+        "reduce_weights",
+    )
+    layer_output = (inputs + branch_own.astype(f32) + (bias_dense + bias_down)).astype(bf16)
     cotangent_own = cotangent[0].astype(f32)
     grad_inputs, grad_gain, grad_shift = norm_pull(grad_normed_own)
     input_grad = grad_inputs + cotangent_own
@@ -1196,9 +1410,6 @@
     )
 
 
-contract_rows_cols = (((0,), (1,)), ((), ()))
-
-
 def solution(mesh):
     placed = (
         P("fsdp", ("ctx", "tp"), None),

time: 762 us -> 546 us (0.72)
  matrix products: 131 us -> 24.5 us
  Pallas kernels: 537 us -> 450 us
  waiting for transfers between devices: 32.3 us -> 0.77 us
  between operations: 1.69 us -> 14.4 us
    dot_general x9 -> x0, matrix products: 110 us -> none  [the longest x1 18.3 us: body(): jnp.dot(cotangent_rows, down_full, preferred_element_type=f32)]
    pallas_call x2 -> x1, Pallas kernels: 181 us -> 108 us  [gather(): pl.pallas_call(kernel, out_shape=tuple(shapes), in_specs=[ANY] * (line_co...]
    ppermute x4 -> x0, waiting for transfers between devices: 32.3 us -> none  [keep_and_swap(): return (kept, lax.ppermute(sent, 'ctx', swap))]
    pallas_call x1, Pallas kernels: 30.3 us -> 11.6 us  [small_reduce(): pl.pallas_call(kernel, out_shape=jax.ShapeDtypeStruct(block, f32), in_spe...]
    pallas_call x3 -> x6, Pallas kernels: 317 us -> 322 us  [the longest x1 110 us: reduce(): pl.pallas_call(kernel, out_shape=tuple(shapes + made_shapes), in_specs=[A...]
    unnamed x82 -> x48, local copies, waits for them, and re-layouts: 12.1 us -> 15.6 us
  transfers between devices with their start and end apart: 4 -> 4, of which waited for: 1 -> 0; matrix products, arithmetic and copies ran while one was open for 14% -> 6% of each run, Pallas kernels for 25% -> 73%
where the time goes in v2:
time: 546 us; the launch traced here: 541 us
  Pallas kernels  450 us (82%)
  local copies, waits for them, and re-layouts  27.3 us (5%)
  matrix products  24.5 us (4%)
  other arithmetic  23.8 us (4%)
  between operations  14.4 us (3%)
    pallas_call x1, Pallas kernels, reduce(): pl.pallas_call(kernel, out_shape=tuple(shapes + made_shapes), in_specs=[A...  110 us
    pallas_call x1, Pallas kernels, gather(): pl.pallas_call(kernel, out_shape=tuple(shapes), in_specs=[ANY] * (line_co...  108 us
    pallas_call x1, Pallas kernels, exchange_back(): pl.pallas_call(kernel, out_shape=(jax.ShapeDtypeStruct((kinds, 2 * width,...  70.3 us
    pallas_call x1, Pallas kernels, exchange_forward(): pl.pallas_call(kernel, out_shape=(jax.ShapeDtypeStruct((2, kinds, count,...  50 us
    pallas_call x1, Pallas kernels, attend_back(): pl.pallas_call(attend_back_kernel, out_shape=jax.ShapeDtypeStruct((3, wid...  38.2 us
    pallas_call x1, Pallas kernels, exchange_middle(): pl.pallas_call(kernel, out_shape=(jax.ShapeDtypeStruct((2 * width, length...  33.8 us
    pallas_call x1, Pallas kernels, attend(): pl.pallas_call(attend_kernel, out_shape=(jax.ShapeDtypeStruct((width, tot...  20.2 us
    unnamed x48, local copies, waits for them, and re-layouts  15.6 us
  transfers between devices with their start and end apart: 4, of which 0 were waited for; matrix products, arithmetic and copies ran while one was open for 6% of the time, Pallas kernels for 73%

profile of v2, /device:TPU:0, one launch (start us, length us, event | category | flops | bytes accessed | tf_op | source)
XLA Modules:
  0.0 540.8 jit_solution(4860834367262431249)
XLA Ops:
  10.0 1.4 convert_reduce_fusion.4
  11.4 1.6 fusion.10
  14.3 8.3 %small_gather.1 = (f32[8,8,256]{2,1,0:T(8,128)}, s32[8,1024]{1,0:T(8,128)}) custom-call(f32[8,256]{1,0:T(8,128)} %fusion.27.block_ref, s32[8,1024]{1,0:T(8,128)} %pad.14.pair_ref), custom_call_target="tpu_custom_call" | custom-call | tf_op jit(solution)/shard_map/small_gather/pallas_call | solution.py:175
  23.8 1.4 fusion.9
  28.0 1.2 copy.29.refs_0_
  29.1 107.8 %gather_weights.1 = (bf16[2048,1536]{1,0:T(8,128)(2,1)}, bf16[2048,2048]{1,0:T(8,128)(2,1)}, bf16[2048,512]{1,0:T(8,128)(2,1)}, bf16[2048,2048]{1,0:T(8,128)(2,1)}) custom-call(bf16[256,1536]{1,0:T(8,128)(2,1)} %copy.29.refs_0_, bf16[256,2048]{1,0:T(8,128)(2,1)} %refs_1_.1, bf16[256,512]{1,0:T(8,128)(2,1)} %refs_2_.1, bf16[256,2048]{1,0:T(8,128)(2,1)} %refs_3_.1), custom_call_target="tpu_custom_call" | custom-call | bytes 380000000 | tf_op jit(solution)/shard_map/gather_weights/pallas_call | solution.py:408
  137.6 10.8 %convolution_add_fusion = f32[1536,1024]{1,0:T(8,128)S(1)} fusion(bf16[2048,1536]{1,0:T(8,128)(2,1)} %get-tuple-element.42.weight_ref, bf16[1024,2048]{1,0:T(8,128)(2,1)} %all-gather.4.cloned.1.call-done.normed_ref.refs_2_, f32[1536]{0:T(1024)S(1)} %reshape.170), kind=kOutput, calls=%fused_computation.3 | convolution fusion | flops 6444023808 | bytes 16783360 | tf_op jit(solution)/shard_map/dot_general | solution.py:1336
  149.6 1.9 pad_maximum_fusion.triple_ref
  151.5 50.0 %exchange_forward.1 = (bf16[2,3,256,1024]{3,2,1,0:T(8,128)(2,1)}, bf16[1024,2048]{1,0:T(8,128)(2,1)}, bf16[1024,2048]{1,0:T(8,128)(2,1)}, f32[1024,2048]{1,0:T(8,128)}) custom-call(bf16[3,512,1024]{2,1,0:T(8,128)(2,1)} %pad_maximum_fusion.triple_ref, bf16[1024,2048]{1,0:T(8,128)(2,1)} %all-gather.4.cloned.1.call-done.normed_ref.refs_2_, ...), custom_call_target="tpu_custom_call" | custom-call | bytes 130000000 | tf_op jit(solution)/shard_map/exchange_forward/pallas_call | solution.py:743
  201.5 1.9 copy-done.3
  203.4 20.2 %attend.1 = (bf16[256,2048]{1,0:T(8,128)(2,1)S(1)}, f32[4,1,2048]{2,1,0:T(1,128)S(1)}) custom-call(s32[8]{0:T(128)S(1)} %get-tuple-element.98.low_ref, s32[8]{0:T(128)S(1)} %get-tuple-element.97.mid_ref, bf16[2,3,256,1024]{3,2,1,0:T(8,128)(2,1)S(1)} %copy-done.3, s32[1,2048]{1,0:T(1,128)S(1)} %bitcast.90), custom_call_target="tpu_custom_call" | custom-call | flops 17895692288 | bytes 4194304 | tf_op jit(solution)/shard_map/attend/pallas_call | solution.py:1205
  224.5 5.5 %convolution_convert_fusion.grad_ref = bf16[512,1024]{1,0:T(8,128)(2,1)} fusion(bf16[2048,512]{1,0:T(8,128)(2,1)S(1)} %copy-done.20, bf16[1024,2048]{1,0:T(8,128)(2,1)} %bitcast.92), kind=kOutput, calls=%fused_computation.33 | convolution fusion | flops 2148007936 | bytes 7340032 | tf_op jit(solution)/shard_map/dot_general | solution.py:1348
  230.1 33.8 %exchange_middle.1 = (bf16[512,1024]{1,0:T(8,128)(2,1)}, bf16[2,256,1024]{2,1,0:T(8,128)(2,1)}, bf16[1024,2048]{1,0:T(8,128)(2,1)}) custom-call(bf16[256,2048]{1,0:T(8,128)(2,1)} %copy-done.1, bf16[512,1024]{1,0:T(8,128)(2,1)} %convolution_convert_fusion.grad_ref, bf16[1024,2048]{1,0:T(8,128)(2,1)} %bitcast.93, ...), custom_call_target="tpu_custom_call" | custom-call | bytes 90000000 | tf_op jit(solution)/shard_map/exchange_middle/pallas_call | solution.py:810
  263.9 8.2 %add_convert_fusion = bf16[1024,2048]{1,0:T(8,128)(2,1)} fusion(f32[1024,2048]{1,0:T(8,128)} %get-tuple-element.54, bf16[512,1024]{1,0:T(8,128)(2,1)} %get-tuple-element.53.refs_5_, bf16[2048,512]{1,0:T(8,128)(2,1)S(1)} %copy-done.20), kind=kOutput, calls=%fused_computation.1 | convolution fusion | flops 2151677952 | bytes 15728640 | tf_op jit(solution)/shard_map/dot_general | solution.py:1355
  272.1 1.1 copy-done.2
  273.6 38.2 %attend_back.1.back_ref = bf16[3,256,2048]{2,1,0:T(8,128)(2,1)S(1)} custom-call(s32[8]{0:T(128)S(1)} %get-tuple-element.98.low_ref, s32[8]{0:T(128)S(1)} %get-tuple-element.97.mid_ref, bf16[2,3,256,1024]{3,2,1,0:T(8,128)(2,1)} %get-tuple-element.46.triple_ref, bf16[2,256,1024]{2,1,0:T(8,128)(2,1)S(1)} %copy-done.4, bf16[256,2048]{1,0:T(8,128)(2,1)S(1)} %copy-done.2, ...), custom_call_target="tpu_custom_call" | custom-call | flops 35791384576 | bytes 6291456 | tf_op jit(solution)/shard_map/attend_back/pallas_call | solution.py:1227
  311.8 1.7 copy-done
  313.5 70.3 %exchange_back.1 = (bf16[3,512,1024]{2,1,0:T(8,128)(2,1)}, bf16[1024,2048]{1,0:T(8,128)(2,1)}, bf16[1024,2048]{1,0:T(8,128)(2,1)}, bf16[1024,2048]{1,0:T(8,128)(...) custom-call(bf16[3,256,2048]{2,1,0:T(8,128)(2,1)} %copy-done, ...), custom_call_target="tpu_custom_call" | custom-call | bytes 220000000 | tf_op jit(solution)/shard_map/exchange_back/pallas_call | solution.py:913
  383.9 1.2 copy-done.6
  385.3 2.4 convert_reduce_fusion.1
  387.6 3.1 convert_reduce_fusion
  391.4 109.6 %reduce_weights.1 = (f32[256,2048]{1,0:T(8,128)}, f32[256,2048]{1,0:T(8,128)}, f32[256,1536]{1,0:T(8,128)}, f32[256,512]{1,0:T(8,128)}, f32[28,128]{1,0:T(8,128)...) custom-call(bf16[4,256,2048]{2,1,0:T(8,128)(2,1)} %bitcast.101, bf16[4,256,2048]{2,1,0:T(8,128)(2,1)} %bitcast.102, ...), custom_call_target="tpu_custom_call" | custom-call | bytes 400000000 | tf_op jit(solution)/shard_map/reduce_weights/pallas_call | solution.py:665
  501.0 3.0 copy.30
  504.1 3.0 copy.31
  508.3 1.9 fusion.11
  510.2 1.1 fusion.16
  511.9 11.6 %small_reduce.1 = f32[8,256]{1,0:T(8,128)} custom-call(f32[8,8,256]{2,1,0:T(8,128)} %pad.17.blocks_ref), custom_call_target="tpu_custom_call" | custom-call | tf_op jit(solution)/shard_map/small_reduce/pallas_call | solution.py:980
  523.5 1.4 fusion.29
  524.9 4.1 fusion.15
  530.4 1.3 copy.38
  531.7 1.0 copy-done.8
  532.8 1.3 copy.39
  (95 shorter events, 15.0 us)
Async XLA Ops:
  7.2 16.5 %copy-start.5 = (bf16[1,256,2048]{2,1,0:T(8,128)(2,1)S(1)}, bf16[1,256,2048]{2,1,0:T(8,128)(2,1)}, u32[]{:S(2)}) copy-start(bf16[1,256,2048]{2,1,0:T(8,128)(2,1)} %param.14) | copy-start | bytes 3145732
  7.2 5.9 %copy-start.18 = (s32[1,1024]{1,0:T(1,128)S(1)}, s32[1,1024]{1,0:T(1,128)}, u32[]{:S(2)}) copy-start(s32[1,1024]{1,0:T(1,128)} %param.16) | copy-start | bytes 12292
  7.2 5.9 %copy-start.19 = (s32[1,1024]{1,0:T(1,128)S(1)}, s32[1,1024]{1,0:T(1,128)}, u32[]{:S(2)}) copy-start(s32[1,1024]{1,0:T(1,128)} %param.15) | copy-start | bytes 12292
  7.2 130.4 %all-gather.4.cloned.1.call-start = ((), (), s32[]{:S(2)}) async-start(), calls=%async_computation.2 | async-start | bytes 5242880 | tf_op jit(solution)/shard_map/all_gather | solution.py:1322
  23.7 2.3 copy-start.12
  23.7 2.3 copy-start.13
  23.7 3.3 copy-start.15
  23.8 3.3 copy-start.16
  23.8 3.9 copy-start.10
  25.2 199.3 %all-gather.6.cloned.1.call-start = ((), (), s32[]{:S(2)}) async-start(), calls=%async_computation.5 | async-start | bytes 5242880 | tf_op jit(solution)/shard_map/all_gather | solution.py:1335
  26.0 357.9 %reduce-scatter.3.cloned.1.call-start = ((), (), s32[]{:S(2)}) async-start(), calls=%async_computation.3 | async-start | bytes 5242880 | tf_op jit(solution)/shard_map/reduce_scatter | solution.py:1357
  201.5 1.9 copy-start.3
  203.4 21.2 %copy-start.20 = (bf16[2048,512]{1,0:T(8,128)(2,1)S(1)}, bf16[2048,512]{1,0:T(8,128)(2,1)}, u32[]{:S(2)}) copy-start(bf16[2048,512]{1,0:T(8,128)(2,1)} %get-tuple-element.48) | copy-start | bytes 6291460
  223.6 1.0 copy-start.1
  272.0 1.2 copy-start.2
  272.0 1.5 copy-start.4
  272.1 236.3 %reduce-scatter.5.cloned.1.call-start = ((), (), s32[]{:S(2)}) async-start(), calls=%async_computation.4 | async-start | bytes 5242880 | tf_op jit(solution)/shard_map/reduce_scatter | solution.py:1375
  311.8 1.7 copy-start
  383.9 1.2 copy-start.6
  504.0 3.0 copy-start.14
  508.3 1.9 copy-start.7
  524.9 4.2 copy-start.17
  524.9 4.7 copy-start.11
  524.9 5.5 %copy-start.9 = (f32[256,2048]{1,0:T(8,128)S(1)}, f32[256,2048]{1,0:T(8,128)}, u32[]{:S(2)}) copy-start(f32[256,2048]{1,0:T(8,128)} %get-tuple-element.157) | copy-start | bytes 6291460
  530.4 2.3 copy-start.8
Sparse Core Ops, SparseCore 0:
  25.4 81.3 all-gather.3
  108.3 79.2 all-gather.5
  272.2 76.6 reduce-scatter.2
  384.0 76.3 reduce-scatter.4
